TPU v7x, 512 devices: a whole 4x4x16 slice. The times are simulated.
512 devices in a mesh: gx: 16 (over z), gy: 8 (over y, core), gz: 4 (over x).
Axes of the slice: x: 4, y: 4, z: 16, core: 2. Of those that a mesh axis runs over, the one named last changes fastest.
Arguments:
- right_side: float32 [4, 32, 512, 1024], P(None, 'gz', 'gx', 'gy'), may hold values from -108 to 108
- start_guess: float32 [4, 32, 512, 1024], P(None, 'gz', 'gx', 'gy'), may hold values from -6 to 6
- diagonal: float32 [32, 512, 1024], P('gz', 'gx', 'gy'), may hold values from 0.25 to 2
Outputs:
- ortho_basis: float32 [16, 32, 512, 1024], P(None, 'gz', 'gx', 'gy')
- rfactor: float32 [16, 16], replicated
All inputs are finite; a program needn't handle non-finite values.
Results may differ from a plain program's by a relative error of at most 0.0003.
Values sent between devices are 32-bit elements; how exact they have to be, the bound alone decides.
A program may use at most 64 MiB of HBM per device.

v0:
```python
import jax
import jax.numpy as jnp
from jax import lax
from jax.sharding import PartitionSpec as P

POWERS = 4


shift_value = 7.125
scale_value = 3.0


def with_halo(block, sides, width):
    for axis, dim in sides:
        count = lax.axis_size(axis)
        forward = [(i, i + 1) for i in range(count - 1)]
        backward = [(target, source) for source, target in forward]
        low = lax.ppermute(
            lax.slice_in_dim(block, block.shape[dim] - width, None, axis=dim), axis, forward
        )
        high = lax.ppermute(lax.slice_in_dim(block, 0, width, axis=dim), axis, backward)
        block = jnp.concatenate([low, block, high], axis=dim)
    return block


def stencil(padded, diag_core):
    interior = padded[:, 1:-1, 1:-1, 1:-1]
    beside = padded[:, 2:, 1:-1, 1:-1] + padded[:, :-2, 1:-1, 1:-1]
    beside = beside + padded[:, 1:-1, 2:, 1:-1] + padded[:, 1:-1, :-2, 1:-1]
    beside = beside + padded[:, 1:-1, 1:-1, 2:] + padded[:, 1:-1, 1:-1, :-2]
    return (6.0 + diag_core) * interior - beside


def upper_factor(gram):
    count = gram.shape[0]
    places = jnp.arange(count)
    rows = []
    for index in range(count):
        rest = gram[index]
        if index > 0:
            earlier = jnp.stack(rows, 0)
            rest = rest - jnp.dot(earlier[:, index], earlier, precision=lax.Precision.HIGHEST)
        pivot = jnp.sqrt(rest[index])
        rows.append(jnp.where(places >= index, rest / pivot, jnp.zeros_like(rest)))
    return jnp.stack(rows, 0)


def upper_inverse(upper):
    count = upper.shape[0]
    identity = jnp.eye(count, dtype=upper.dtype)
    solved = [None] * count
    for index in reversed(range(count)):
        accum = identity[index]
        if index < count - 1:
            later = jnp.stack(solved[index + 1 :], 0)
            accum = accum - jnp.dot(
                upper[index, index + 1 :], later, precision=lax.Precision.HIGHEST
            )
        solved[index] = accum / upper[index, index]
    return jnp.stack(solved, 0)


def apply_once(field, diagonal):
    padded = with_halo(field, (("gx", 2), ("gy", 3), ("gz", 1)), 1)
    return stencil(padded, diagonal)


def local(right_side, start_guess, diagonal):
    nrhs = right_side.shape[0]
    zlen, xlen, ylen = (right_side.shape[1], right_side.shape[2], right_side.shape[3])
    residual = right_side - apply_once(start_guess, diagonal)
    columns = [residual]
    vector = residual
    for power in range(POWERS - 1):
        vector = (apply_once(vector, diagonal) - shift_value * vector) / scale_value
        columns.append(vector)
    width = nrhs * POWERS
    basis = jnp.concatenate(columns, 0).reshape(width, -1)
    local_gram = jnp.dot(basis, basis.T, precision=lax.Precision.HIGHEST)
    gram = lax.psum(local_gram, ("gx", "gy", "gz"))
    rfactor = upper_factor(gram)
    inverse = upper_inverse(rfactor)
    ortho = jnp.dot(inverse.T, basis, precision=lax.Precision.HIGHEST)
    return (ortho.reshape(width, zlen, xlen, ylen), rfactor)


def solution(mesh):
    placed = (P(None, "gz", "gx", "gy"), P(None, "gz", "gx", "gy"), P("gz", "gx", "gy"))
    return jax.shard_map(
        local,
        mesh=mesh,
        in_specs=placed,
        out_specs=(P(None, "gz", "gx", "gy"), P()),
        check_vma=False,
    )
```

profile of v0, /device:TPU:1, one launch (start us, length us, event | category | flops | bytes accessed | tf_op | source)
XLA Modules:
  0.0 303.7 jit_solution(15568385002712104598)
XLA Ops:
  2.0 4.4 %collective-permute-start = (f32[4,8,1,128]{3,0,2,1:T(4,128)S(1)}, f32[4,8,1,128]{3,0,2,1:T(4,128)S(1)}, u32[]{:S(2)}, u32[]{:S(2)}) collective-permute-start(f32[4,8,1,128]{3,0,2,1:T(4,128)S(1)} %get-tuple-element.51), channel_id=1, source_target_pairs={{0,32},{32,64},{64,96},{96,128},{128,160},{160,192},{192,224},{224... | collective-permute-start | bytes 49160 | tf_op jit(solution)/shard_map/ppermute | solution.py:18
  11.8 5.0 %collective-permute-start.2 = (f32[4,8,34,1]{2,1,3,0:T(8,128)S(1)}, f32[4,8,34,1]{2,1,3,0:T(8,128)S(1)}, u32[]{:S(2)}, u32[]{:S(2)}) collective-permute-start(f32[4,8,34,1]{2,1,3,0:T(8,128)S(1)} %copy.237), channel_id=1, source_target_pairs={{0,4},{4,8},{8,12},{12,16},{16,20},{20,24},{24,28},{1,5},{5,9},{9,... | collective-permute-start | bytes 13064 | tf_op jit(solution)/shard_map/ppermute | solution.py:18
  17.1 2.9 collective-permute-start.3
  24.1 4.0 %collective-permute-start.5 = (f32[4,1,34,130]{3,0,2,1:T(4,128)S(1)}, f32[4,1,34,130]{3,0,2,1:T(4,128)S(1)}, u32[]{:S(2)}, u32[]{:S(2)}) collective-permute-start(f32[4,1,34,130]{3,0,2,1:T(4,128)S(1)} %get-tuple-element.35), channel_id=1, source_target_pairs={{0,1},{1,2},{2,3},{4,5},{5,6},{6,7},{8,9},{9,10},{10,11},{12,13},{... | collective-permute-start | bytes 212168 | tf_op jit(solution)/shard_map/ppermute | solution.py:18
  37.7 4.5 %collective-permute-done.7 = f32[4,8,1,128]{3,0,2,1:T(4,128)S(1)} collective-permute-done((f32[4,8,1,128]{3,0,2,1:T(4,128)S(1)}, f32[4,8,1,128]{3,0,2,1:T(4,128)S(1)}, u32[]{:S(2)}, u32[]{:S(2)}) %collective-permute-start.7) | collective-permute-done | bytes 16416 | tf_op jit(solution)/shard_map/ppermute | solution.py:21
  43.0 5.1 %collective-permute-start.8 = (f32[4,8,34,1]{2,1,3,0:T(8,128)S(1)}, f32[4,8,34,1]{2,1,3,0:T(8,128)S(1)}, u32[]{:S(2)}, u32[]{:S(2)}) collective-permute-start(f32[4,8,34,1]{2,1,3,0:T(8,128)S(1)} %copy.246), channel_id=1, source_target_pairs={{0,4},{4,8},{8,12},{12,16},{16,20},{20,24},{24,28},{1,5},{5,9},{9,... | collective-permute-start | bytes 13064 | tf_op jit(solution)/shard_map/ppermute | solution.py:18
  50.8 2.8 collective-permute-done.9
  55.5 4.7 %collective-permute-start.11 = (f32[4,1,34,130]{3,0,2,1:T(4,128)S(1)}, f32[4,1,34,130]{3,0,2,1:T(4,128)S(1)}, u32[]{:S(2)}, u32[]{:S(2)}) collective-permute-start(f32[4,1,34,130]{3,0,2,1:T(4,128)S(1)} %get-tuple-element.33), channel_id=1, source_target_pairs={{0,1},{1,2},{2,3},{4,5},{5,6},{6,7},{8,9},{9,10},{10,11},{12,13},{... | collective-permute-start | bytes 212168 | tf_op jit(solution)/shard_map/ppermute | solution.py:18
  62.2 2.7 broadcast_multiply_fusion.1
  64.9 4.8 %collective-permute-start.12 = (f32[4,8,1,128]{3,0,2,1:T(4,128)S(1)}, f32[4,8,1,128]{3,0,2,1:T(4,128)S(1)}, u32[]{:S(2)}, u32[]{:S(2)}) collective-permute-start(f32[4,8,1,128]{3,0,2,1:T(4,128)S(1)} %get-tuple-element.46), channel_id=1, source_target_pairs={{0,32},{32,64},{64,96},{96,128},{128,160},{160,192},{192,224},{224... | collective-permute-start | bytes 49160 | tf_op jit(solution)/shard_map/ppermute | solution.py:18
  71.1 3.5 %collective-permute-done.13 = f32[4,8,1,128]{3,0,2,1:T(4,128)S(1)} collective-permute-done((f32[4,8,1,128]{3,0,2,1:T(4,128)S(1)}, f32[4,8,1,128]{3,0,2,1:T(4,128)S(1)}, u32[]{:S(2)}, u32[]{:S(2)}) %collective-permute-start.13) | collective-permute-done | bytes 16416 | tf_op jit(solution)/shard_map/ppermute | solution.py:21
  75.3 4.6 %collective-permute-start.14 = (f32[4,8,34,1]{2,1,3,0:T(8,128)S(1)}, f32[4,8,34,1]{2,1,3,0:T(8,128)S(1)}, u32[]{:S(2)}, u32[]{:S(2)}) collective-permute-start(f32[4,8,34,1]{2,1,3,0:T(8,128)S(1)} %copy.252), channel_id=1, source_target_pairs={{0,4},{4,8},{8,12},{12,16},{16,20},{20,24},{24,28},{1,5},{5,9},{9,... | collective-permute-start | bytes 13064 | tf_op jit(solution)/shard_map/ppermute | solution.py:18
  82.6 2.8 collective-permute-done.15
  87.3 4.6 %collective-permute-start.17 = (f32[4,1,34,130]{3,0,2,1:T(4,128)S(1)}, f32[4,1,34,130]{3,0,2,1:T(4,128)S(1)}, u32[]{:S(2)}, u32[]{:S(2)}) collective-permute-start(f32[4,1,34,130]{3,0,2,1:T(4,128)S(1)} %get-tuple-element.31), channel_id=1, source_target_pairs={{0,1},{1,2},{2,3},{4,5},{5,6},{6,7},{8,9},{9,10},{10,11},{12,13},{... | collective-permute-start | bytes 212168 | tf_op jit(solution)/shard_map/ppermute | solution.py:18
  93.9 3.4 %broadcast_multiply_fusion = (f32[4,8,32,128]{3,0,2,1:T(4,128)S(1)}, f32[4,8,32,128]{3,0,2,1:T(4,128)}) fusion(f32[4,8,32,128]{3,0,2,1:T(4,128)S(1)} %get-tuple-element.27, f32[4,8,1,128]{3,0,2,1:T(4,128)S(1)} %collective-permute-done.13, f32[4,8,32,128]{3,0,2,1:T(4,128)S(1)} %get-tuple-element.26, f32[4,8,1,128]{3,0,2,1:T(4,128)S(1)} %collective-permute-done.12, ...), kind=kLoop, calls=%fused_computation.185 | loop fusion | flops 3670016 | bytes 2411136 | tf_op jit(solution)/shard_map/div | solution.py:75
  97.3 3.6 %collective-permute-start.18 = (f32[4,8,1,128]{3,0,2,1:T(4,128)S(1)}, f32[4,8,1,128]{3,0,2,1:T(4,128)S(1)}, u32[]{:S(2)}, u32[]{:S(2)}) collective-permute-start(f32[4,8,1,128]{3,0,2,1:T(4,128)S(1)} %get-tuple-element.44), channel_id=1, source_target_pairs={{0,32},{32,64},{64,96},{96,128},{128,160},{160,192},{192,224},{224... | collective-permute-start | bytes 49160 | tf_op jit(solution)/shard_map/ppermute | solution.py:18
  102.3 3.4 %collective-permute-done.19 = f32[4,8,1,128]{3,0,2,1:T(4,128)S(1)} collective-permute-done((f32[4,8,1,128]{3,0,2,1:T(4,128)S(1)}, f32[4,8,1,128]{3,0,2,1:T(4,128)S(1)}, u32[]{:S(2)}, u32[]{:S(2)}) %collective-permute-start.19) | collective-permute-done | bytes 16416 | tf_op jit(solution)/shard_map/ppermute | solution.py:21
  106.4 4.7 %collective-permute-start.20 = (f32[4,8,34,1]{2,1,3,0:T(8,128)S(1)}, f32[4,8,34,1]{2,1,3,0:T(8,128)S(1)}, u32[]{:S(2)}, u32[]{:S(2)}) collective-permute-start(f32[4,8,34,1]{2,1,3,0:T(8,128)S(1)} %copy.258), channel_id=1, source_target_pairs={{0,4},{4,8},{8,12},{12,16},{16,20},{20,24},{24,28},{1,5},{5,9},{9,... | collective-permute-start | bytes 13064 | tf_op jit(solution)/shard_map/ppermute | solution.py:18
  118.5 5.2 %collective-permute-start.23 = (f32[4,1,34,130]{3,0,2,1:T(4,128)S(1)}, f32[4,1,34,130]{3,0,2,1:T(4,128)S(1)}, u32[]{:S(2)}, u32[]{:S(2)}) collective-permute-start(f32[4,1,34,130]{3,0,2,1:T(4,128)S(1)} %get-tuple-element.29), channel_id=1, source_target_pairs={{0,1},{1,2},{2,3},{4,5},{5,6},{6,7},{8,9},{9,10},{10,11},{12,13},{... | collective-permute-start | bytes 212168 | tf_op jit(solution)/shard_map/ppermute | solution.py:18
  125.7 2.7 fusion.61
  129.1 2.9 convolution_bitcast_fusion
  132.0 106.5 %psum.7 = f32[16,16]{1,0:T(8,128)S(1)} all-reduce(f32[16,16]{1,0:T(8,128)S(1)} %convolution_bitcast_fusion), channel_id=1, replica_groups=mesh['gx'=16,'gy'=8,'gz'=4] {'gx','gy','gz'}, use_global_device_ids=true, to_apply=%region_0.0 | all-reduce | flops 256 | bytes 2048 | tf_op jit(solution)/shard_map/psum | solution.py:80
  275.8 2.9 pad_maximum_fusion
  298.9 2.8 fusion
  (214 shorter events, 96.9 us)
Async XLA Ops:
  2.0 5.7 %collective-permute-start = (f32[4,8,1,128]{3,0,2,1:T(4,128)S(1)}, f32[4,8,1,128]{3,0,2,1:T(4,128)S(1)}, u32[]{:S(2)}, u32[]{:S(2)}) collective-permute-start(f32[4,8,1,128]{3,0,2,1:T(4,128)S(1)} %get-tuple-element.51), channel_id=1, source_target_pairs={{0,32},{32,64},{64,96},{96,128},{128,160},{160,192},{192,224},{224... | collective-permute-start | bytes 49160 | tf_op jit(solution)/shard_map/ppermute | solution.py:18
  6.4 4.7 %collective-permute-start.1 = (f32[4,8,1,128]{3,0,2,1:T(4,128)S(1)}, f32[4,8,1,128]{3,0,2,1:T(4,128)S(1)}, u32[]{:S(2)}, u32[]{:S(2)}) collective-permute-start(f32[4,8,1,128]{3,0,2,1:T(4,128)S(1)} %get-tuple-element.50), channel_id=1, source_target_pairs={{32,0},{64,32},{96,64},{128,96},{160,128},{192,160},{224,192},{256... | collective-permute-start | bytes 49160 | tf_op jit(solution)/shard_map/ppermute | solution.py:21
  11.8 8.3 %collective-permute-start.2 = (f32[4,8,34,1]{2,1,3,0:T(8,128)S(1)}, f32[4,8,34,1]{2,1,3,0:T(8,128)S(1)}, u32[]{:S(2)}, u32[]{:S(2)}) collective-permute-start(f32[4,8,34,1]{2,1,3,0:T(8,128)S(1)} %copy.237), channel_id=1, source_target_pairs={{0,4},{4,8},{8,12},{12,16},{16,20},{20,24},{24,28},{1,5},{5,9},{9,... | collective-permute-start | bytes 13064 | tf_op jit(solution)/shard_map/ppermute | solution.py:18
  17.1 5.1 %collective-permute-start.3 = (f32[4,8,34,1]{2,1,3,0:T(8,128)S(1)}, f32[4,8,34,1]{2,1,3,0:T(8,128)S(1)}, u32[]{:S(2)}, u32[]{:S(2)}) collective-permute-start(f32[4,8,34,1]{2,1,3,0:T(8,128)S(1)} %copy.238), channel_id=1, source_target_pairs={{4,0},{8,4},{12,8},{16,12},{20,16},{24,20},{28,24},{5,1},{9,5},{13... | collective-permute-start | bytes 13064 | tf_op jit(solution)/shard_map/ppermute | solution.py:21
  22.8 6.8 %collective-permute-start.4 = (f32[4,1,34,130]{3,0,2,1:T(4,128)S(1)}, f32[4,1,34,130]{3,0,2,1:T(4,128)S(1)}, u32[]{:S(2)}, u32[]{:S(2)}) collective-permute-start(f32[4,1,34,130]{3,0,2,1:T(4,128)S(1)} %get-tuple-element.34), channel_id=1, source_target_pairs={{1,0},{2,1},{3,2},{5,4},{6,5},{7,6},{9,8},{10,9},{11,10},{13,12},{... | collective-permute-start | bytes 212168 | tf_op jit(solution)/shard_map/ppermute | solution.py:21
  24.1 7.3 %collective-permute-start.5 = (f32[4,1,34,130]{3,0,2,1:T(4,128)S(1)}, f32[4,1,34,130]{3,0,2,1:T(4,128)S(1)}, u32[]{:S(2)}, u32[]{:S(2)}) collective-permute-start(f32[4,1,34,130]{3,0,2,1:T(4,128)S(1)} %get-tuple-element.35), channel_id=1, source_target_pairs={{0,1},{1,2},{2,3},{4,5},{5,6},{6,7},{8,9},{9,10},{10,11},{12,13},{... | collective-permute-start | bytes 212168 | tf_op jit(solution)/shard_map/ppermute | solution.py:18
  33.9 3.8 %collective-permute-start.6 = (f32[4,8,1,128]{3,0,2,1:T(4,128)S(1)}, f32[4,8,1,128]{3,0,2,1:T(4,128)S(1)}, u32[]{:S(2)}, u32[]{:S(2)}) collective-permute-start(f32[4,8,1,128]{3,0,2,1:T(4,128)S(1)} %get-tuple-element.48), channel_id=1, source_target_pairs={{0,32},{32,64},{64,96},{96,128},{128,160},{160,192},{192,224},{224... | collective-permute-start | bytes 49160 | tf_op jit(solution)/shard_map/ppermute | solution.py:18
  36.4 5.8 %collective-permute-start.7 = (f32[4,8,1,128]{3,0,2,1:T(4,128)S(1)}, f32[4,8,1,128]{3,0,2,1:T(4,128)S(1)}, u32[]{:S(2)}, u32[]{:S(2)}) collective-permute-start(f32[4,8,1,128]{3,0,2,1:T(4,128)S(1)} %get-tuple-element.49), channel_id=1, source_target_pairs={{32,0},{64,32},{96,64},{128,96},{160,128},{192,160},{224,192},{256... | collective-permute-start | bytes 49160 | tf_op jit(solution)/shard_map/ppermute | solution.py:21
  43.0 7.4 %collective-permute-start.8 = (f32[4,8,34,1]{2,1,3,0:T(8,128)S(1)}, f32[4,8,34,1]{2,1,3,0:T(8,128)S(1)}, u32[]{:S(2)}, u32[]{:S(2)}) collective-permute-start(f32[4,8,34,1]{2,1,3,0:T(8,128)S(1)} %copy.246), channel_id=1, source_target_pairs={{0,4},{4,8},{8,12},{12,16},{16,20},{20,24},{24,28},{1,5},{5,9},{9,... | collective-permute-start | bytes 13064 | tf_op jit(solution)/shard_map/ppermute | solution.py:18
  48.5 5.0 %collective-permute-start.9 = (f32[4,8,34,1]{2,1,3,0:T(8,128)S(1)}, f32[4,8,34,1]{2,1,3,0:T(8,128)S(1)}, u32[]{:S(2)}, u32[]{:S(2)}) collective-permute-start(f32[4,8,34,1]{2,1,3,0:T(8,128)S(1)} %copy.247), channel_id=1, source_target_pairs={{4,0},{8,4},{12,8},{16,12},{20,16},{24,20},{28,24},{5,1},{9,5},{13... | collective-permute-start | bytes 13064 | tf_op jit(solution)/shard_map/ppermute | solution.py:21
  54.2 6.5 %collective-permute-start.10 = (f32[4,1,34,130]{3,0,2,1:T(4,128)S(1)}, f32[4,1,34,130]{3,0,2,1:T(4,128)S(1)}, u32[]{:S(2)}, u32[]{:S(2)}) collective-permute-start(f32[4,1,34,130]{3,0,2,1:T(4,128)S(1)} %get-tuple-element.32), channel_id=1, source_target_pairs={{1,0},{2,1},{3,2},{5,4},{6,5},{7,6},{9,8},{10,9},{11,10},{13,12},{... | collective-permute-start | bytes 212168 | tf_op jit(solution)/shard_map/ppermute | solution.py:21
  55.5 6.7 %collective-permute-start.11 = (f32[4,1,34,130]{3,0,2,1:T(4,128)S(1)}, f32[4,1,34,130]{3,0,2,1:T(4,128)S(1)}, u32[]{:S(2)}, u32[]{:S(2)}) collective-permute-start(f32[4,1,34,130]{3,0,2,1:T(4,128)S(1)} %get-tuple-element.33), channel_id=1, source_target_pairs={{0,1},{1,2},{2,3},{4,5},{5,6},{6,7},{8,9},{9,10},{10,11},{12,13},{... | collective-permute-start | bytes 212168 | tf_op jit(solution)/shard_map/ppermute | solution.py:18
  64.9 6.2 %collective-permute-start.12 = (f32[4,8,1,128]{3,0,2,1:T(4,128)S(1)}, f32[4,8,1,128]{3,0,2,1:T(4,128)S(1)}, u32[]{:S(2)}, u32[]{:S(2)}) collective-permute-start(f32[4,8,1,128]{3,0,2,1:T(4,128)S(1)} %get-tuple-element.46), channel_id=1, source_target_pairs={{0,32},{32,64},{64,96},{96,128},{128,160},{160,192},{192,224},{224... | collective-permute-start | bytes 49160 | tf_op jit(solution)/shard_map/ppermute | solution.py:18
  69.8 4.8 %collective-permute-start.13 = (f32[4,8,1,128]{3,0,2,1:T(4,128)S(1)}, f32[4,8,1,128]{3,0,2,1:T(4,128)S(1)}, u32[]{:S(2)}, u32[]{:S(2)}) collective-permute-start(f32[4,8,1,128]{3,0,2,1:T(4,128)S(1)} %get-tuple-element.47), channel_id=1, source_target_pairs={{32,0},{64,32},{96,64},{128,96},{160,128},{192,160},{224,192},{256... | collective-permute-start | bytes 49160 | tf_op jit(solution)/shard_map/ppermute | solution.py:21
  75.3 6.9 %collective-permute-start.14 = (f32[4,8,34,1]{2,1,3,0:T(8,128)S(1)}, f32[4,8,34,1]{2,1,3,0:T(8,128)S(1)}, u32[]{:S(2)}, u32[]{:S(2)}) collective-permute-start(f32[4,8,34,1]{2,1,3,0:T(8,128)S(1)} %copy.252), channel_id=1, source_target_pairs={{0,4},{4,8},{8,12},{12,16},{16,20},{20,24},{24,28},{1,5},{5,9},{9,... | collective-permute-start | bytes 13064 | tf_op jit(solution)/shard_map/ppermute | solution.py:18
  80.3 5.0 %collective-permute-start.15 = (f32[4,8,34,1]{2,1,3,0:T(8,128)S(1)}, f32[4,8,34,1]{2,1,3,0:T(8,128)S(1)}, u32[]{:S(2)}, u32[]{:S(2)}) collective-permute-start(f32[4,8,34,1]{2,1,3,0:T(8,128)S(1)} %copy.253), channel_id=1, source_target_pairs={{4,0},{8,4},{12,8},{16,12},{20,16},{24,20},{28,24},{5,1},{9,5},{13... | collective-permute-start | bytes 13064 | tf_op jit(solution)/shard_map/ppermute | solution.py:21
  86.0 6.4 %collective-permute-start.16 = (f32[4,1,34,130]{3,0,2,1:T(4,128)S(1)}, f32[4,1,34,130]{3,0,2,1:T(4,128)S(1)}, u32[]{:S(2)}, u32[]{:S(2)}) collective-permute-start(f32[4,1,34,130]{3,0,2,1:T(4,128)S(1)} %get-tuple-element.30), channel_id=1, source_target_pairs={{1,0},{2,1},{3,2},{5,4},{6,5},{7,6},{9,8},{10,9},{11,10},{13,12},{... | collective-permute-start | bytes 212168 | tf_op jit(solution)/shard_map/ppermute | solution.py:21
  87.3 6.6 %collective-permute-start.17 = (f32[4,1,34,130]{3,0,2,1:T(4,128)S(1)}, f32[4,1,34,130]{3,0,2,1:T(4,128)S(1)}, u32[]{:S(2)}, u32[]{:S(2)}) collective-permute-start(f32[4,1,34,130]{3,0,2,1:T(4,128)S(1)} %get-tuple-element.31), channel_id=1, source_target_pairs={{0,1},{1,2},{2,3},{4,5},{5,6},{6,7},{8,9},{9,10},{10,11},{12,13},{... | collective-permute-start | bytes 212168 | tf_op jit(solution)/shard_map/ppermute | solution.py:18
  97.3 4.9 %collective-permute-start.18 = (f32[4,8,1,128]{3,0,2,1:T(4,128)S(1)}, f32[4,8,1,128]{3,0,2,1:T(4,128)S(1)}, u32[]{:S(2)}, u32[]{:S(2)}) collective-permute-start(f32[4,8,1,128]{3,0,2,1:T(4,128)S(1)} %get-tuple-element.44), channel_id=1, source_target_pairs={{0,32},{32,64},{64,96},{96,128},{128,160},{160,192},{192,224},{224... | collective-permute-start | bytes 49160 | tf_op jit(solution)/shard_map/ppermute | solution.py:18
  100.9 4.7 %collective-permute-start.19 = (f32[4,8,1,128]{3,0,2,1:T(4,128)S(1)}, f32[4,8,1,128]{3,0,2,1:T(4,128)S(1)}, u32[]{:S(2)}, u32[]{:S(2)}) collective-permute-start(f32[4,8,1,128]{3,0,2,1:T(4,128)S(1)} %get-tuple-element.45), channel_id=1, source_target_pairs={{32,0},{64,32},{96,64},{128,96},{160,128},{192,160},{224,192},{256... | collective-permute-start | bytes 49160 | tf_op jit(solution)/shard_map/ppermute | solution.py:21
  106.4 7.2 %collective-permute-start.20 = (f32[4,8,34,1]{2,1,3,0:T(8,128)S(1)}, f32[4,8,34,1]{2,1,3,0:T(8,128)S(1)}, u32[]{:S(2)}, u32[]{:S(2)}) collective-permute-start(f32[4,8,34,1]{2,1,3,0:T(8,128)S(1)} %copy.258), channel_id=1, source_target_pairs={{0,4},{4,8},{8,12},{12,16},{16,20},{20,24},{24,28},{1,5},{5,9},{9,... | collective-permute-start | bytes 13064 | tf_op jit(solution)/shard_map/ppermute | solution.py:18
  111.5 5.0 %collective-permute-start.21 = (f32[4,8,34,1]{2,1,3,0:T(8,128)S(1)}, f32[4,8,34,1]{2,1,3,0:T(8,128)S(1)}, u32[]{:S(2)}, u32[]{:S(2)}) collective-permute-start(f32[4,8,34,1]{2,1,3,0:T(8,128)S(1)} %copy.259), channel_id=1, source_target_pairs={{4,0},{8,4},{12,8},{16,12},{20,16},{24,20},{28,24},{5,1},{9,5},{13... | collective-permute-start | bytes 13064 | tf_op jit(solution)/shard_map/ppermute | solution.py:21
  117.2 7.0 %collective-permute-start.22 = (f32[4,1,34,130]{3,0,2,1:T(4,128)S(1)}, f32[4,1,34,130]{3,0,2,1:T(4,128)S(1)}, u32[]{:S(2)}, u32[]{:S(2)}) collective-permute-start(f32[4,1,34,130]{3,0,2,1:T(4,128)S(1)} %get-tuple-element.28), channel_id=1, source_target_pairs={{1,0},{2,1},{3,2},{5,4},{6,5},{7,6},{9,8},{10,9},{11,10},{13,12},{... | collective-permute-start | bytes 212168 | tf_op jit(solution)/shard_map/ppermute | solution.py:21
  118.5 7.2 %collective-permute-start.23 = (f32[4,1,34,130]{3,0,2,1:T(4,128)S(1)}, f32[4,1,34,130]{3,0,2,1:T(4,128)S(1)}, u32[]{:S(2)}, u32[]{:S(2)}) collective-permute-start(f32[4,1,34,130]{3,0,2,1:T(4,128)S(1)} %get-tuple-element.29), channel_id=1, source_target_pairs={{0,1},{1,2},{2,3},{4,5},{5,6},{6,7},{8,9},{9,10},{10,11},{12,13},{... | collective-permute-start | bytes 212168 | tf_op jit(solution)/shard_map/ppermute | solution.py:18
  (3 other events, 37.0 us)
where the time goes:
time: 305 us; the launch traced here: 304 us
  blocking collectives  107 us (35%)
  starting transfers between devices  72.6 us (24%)
  local copies, waits for them, and re-layouts  42.3 us (14%)
  waiting for transfers between devices  32.3 us (11%)
  matrix products  19 us (6%)
  other arithmetic  18.7 us (6%)
  between operations  12.4 us (4%)
    psum x1, blocking collectives, local(): gram = lax.psum(local_gram, ('gx', 'gy', 'gz'))  107 us
    ppermute x12, starting transfers between devices, with_halo(): lax.ppermute(lax.slice_in_dim(block, block.shape[dim] - width, None, axis...  53.4 us
    ppermute x12, waiting for transfers between devices, with_halo(): lax.ppermute(lax.slice_in_dim(block, 0, width, axis=dim), axis, backward)  26 us
    ppermute x12, starting transfers between devices, with_halo(): lax.ppermute(lax.slice_in_dim(block, 0, width, axis=dim), axis, backward)  19.2 us
    dot_general x14, matrix products, upper_inverse(): jnp.dot(upper[index, index + 1:], later, precision=lax.Precision.HIGHEST)  11.5 us
    slice x16, local copies, waits for them, and re-layouts, upper_factor(): pivot = jnp.sqrt(rest[index])  9.45 us
    slice x15, local copies, waits for them, and re-layouts, upper_inverse(): solved[index] = accum / upper[index, index]  9.11 us
    div x3, other arithmetic, local(): vector = (apply_once(vector, diagonal) - shift_value * vector) / scale_value  8.7 us
  transfers between devices with their start and end apart: 24, of which 16 were waited for; matrix products, arithmetic and copies ran while one was open for 1% of the time, Pallas kernels for 0%

commit v1 on v0

v1 whole, which is shorter than its diff:
```python
import functools

import jax
import jax.numpy as jnp
from jax import lax
from jax.experimental import pallas as pl
from jax.experimental.pallas import tpu as pltpu
from jax.sharding import PartitionSpec as P

MESH = pl.DeviceIdType.MESH
F32 = jnp.float32
RHS = 4
POWERS = 4
shift_value = 7.125
scale_value = 3.0

PAIRS = [(r, s) for r in range(RHS) for s in range(r, RHS)]
EARLY = [(k, pair) for k in range(5) for pair in PAIRS]
LATE = [(k, pair) for k in (5, 6) for pair in PAIRS]
EARLY_GROUPS = -(-len(EARLY) // 8)
LATE_GROUPS = -(-len(LATE) // 8)
GROUPS = EARLY_GROUPS + LATE_GROUPS
ROW_OF = {entry: row for row, entry in enumerate(EARLY)}
ROW_OF.update({entry: EARLY_GROUPS * 8 + row for row, entry in enumerate(LATE)})


def ring(axis, offset):
    count = lax.axis_size(axis)
    return lax.rem(lax.axis_index(axis) + (offset + count), count)


def far_first(offsets, distance):
    return sorted(offsets, key=lambda k: -distance(k))


def tree_sum(values):
    values = list(values)
    while len(values) > 1:
        values = [
            values[i] + values[i + 1] if i + 1 < len(values) else values[i]
            for i in range(0, len(values), 2)
        ]
    return values[0]


def power_kernel(
    sizes, right_hbm, guess_hbm, diag_hbm, basis_hbm, total_out,
    field, last, right, diag, y_send, y_low, y_high, x_send, x_low, x_high,
    tile0, tile1, tile2, pair_buf, plane_buf, line_buf,
    in_sem, out_sem, halo_send, halo_recv, sum_send, sum_recv,
):
    n_gx, n_gy, n_gz = sizes
    n_y = n_gy // 2
    zlen, xlen = diag.shape[0], diag.shape[1]
    xtiles = xlen // 8
    gx, gy, gz = (lax.axis_index(a) for a in ("gx", "gy", "gz"))

    load_guess = [
        pltpu.make_async_copy(guess_hbm.at[r], field.at[0, r, pl.ds(1, zlen)], in_sem.at[r])
        for r in range(RHS)
    ]
    load_rest = [
        pltpu.make_async_copy(diag_hbm, diag, in_sem.at[RHS]),
        pltpu.make_async_copy(right_hbm, right, in_sem.at[RHS + 1]),
    ]
    for copy in load_guess + load_rest:
        copy.start()

    def dist(k, n):
        return min(k, n - k)

    plane = [(dy, dx) for dy in range(n_y) for dx in range(n_gz) if (dy, dx) != (0, 0)]
    plane = far_first(plane, lambda k: dist(k[0], n_y) + dist(k[1], n_gz))
    line = far_first(range(1, n_gx), lambda k: dist(k, n_gx))

    def plane_dev(k):
        return {"gy": ring("gy", 2 * k[0]), "gz": ring("gz", k[1])}

    barrier = pltpu.get_barrier_semaphore()
    greeted = [{"gy": ring("gy", 1)}, {"gy": ring("gy", -1)}]
    greeted += [plane_dev(k) for k in reversed(plane)]
    greeted += [{"gx": ring("gx", k)} for k in reversed(line)]
    for device in greeted:
        pl.semaphore_signal(barrier, inc=1, device_id=device, device_id_type=MESH)

    lane = lax.broadcasted_iota(jnp.int32, (8, 128), 1)
    sub = lax.broadcasted_iota(jnp.int32, (8, 128), 0)
    lane_half = lane // 2
    odd = lane % 2 == 1
    first_lane, last_lane = lane == 0, lane == 127
    first_row, last_row = sub == 0, sub == 7
    y_has = [(gy > 0).astype(F32), (gy < n_gy - 1).astype(F32)]
    x_has = [(gx > 0).astype(F32), (gx < n_gx - 1).astype(F32)]
    z_has = [(gz > 0).astype(F32), (gz < n_gz - 1).astype(F32)]

    def rows(xt):
        return pl.ds(8 * xt, 8)

    def pack(packed, value, index):
        return jnp.where(lane_half == index, pltpu.roll(value, 2 * index + 1, 1), packed)

    def halo_copies(p, r):
        sends = [
            (field.at[p, r, zlen], field.at[p, r, 0], {"gz": ring("gz", 1)}),
            (field.at[p, r, 1], field.at[p, r, zlen + 1], {"gz": ring("gz", -1)}),
            (x_send.at[p, r, 1], x_low.at[p, r], {"gx": ring("gx", 1)}),
            (x_send.at[p, r, 0], x_high.at[p, r], {"gx": ring("gx", -1)}),
            (y_send.at[p, r], y_low.at[p, r], {"gy": ring("gy", 1)}),
            (y_send.at[p, r], y_high.at[p, r], {"gy": ring("gy", -1)}),
        ]
        return [
            pltpu.make_async_remote_copy(
                src_ref=src, dst_ref=dst, send_sem=halo_send.at[p, r, i],
                recv_sem=halo_recv.at[p, r, i], device_id=device, device_id_type=MESH,
            )
            for i, (src, dst, device) in enumerate(sends)
        ]

    def keep_x_faces(p, r, z, xt, value):
        if xt == 0:
            x_send[p, r, 0, z : z + 1, :] = value[0:1, :]
        if xt == xtiles - 1:
            x_send[p, r, 1, z : z + 1, :] = value[7:8, :]

    for r in range(RHS):
        load_guess[r].wait()
        packed = jnp.zeros((8, 128), F32)
        for z in range(zlen):
            for xt in range(xtiles):
                value = field[0, r, z + 1, rows(xt), :]
                packed = pack(packed, value, z * xtiles + xt)
                keep_x_faces(0, r, z, xt, value)
        y_send[0, r] = packed
        if r == 0:
            pl.semaphore_wait(barrier, len(greeted))
        for copy in halo_copies(0, r):
            copy.start()
    for copy in load_rest:
        copy.wait()

    def step(p, r):
        for copy in halo_copies(p, r):
            copy.wait_recv()
        edges = jnp.where(
            odd, pltpu.roll(y_high[p, r] * y_has[1], 126, 1), y_low[p, r] * y_has[0]
        )
        x_lo = x_low[p, r] * x_has[0]
        x_hi = x_high[p, r] * x_has[1]
        packed = jnp.zeros((8, 128), F32)
        for z in range(zlen):
            for xt in range(xtiles):
                index = z * xtiles + xt
                here = field[p, r, z + 1, rows(xt), :]
                z_lo = field[p, r, z, rows(xt), :]
                z_hi = field[p, r, z + 2, rows(xt), :]
                if z == 0:
                    z_lo = z_lo * z_has[0]
                if z == zlen - 1:
                    z_hi = z_hi * z_has[1]
                if xt == 0:
                    below = jnp.where(first_row, x_lo[z : z + 1, :], pltpu.roll(here, 1, 0))
                else:
                    below = field[p, r, z + 1, pl.ds(8 * xt - 1, 8), :]
                if xt == xtiles - 1:
                    above = jnp.where(last_row, x_hi[z : z + 1, :], pltpu.roll(here, 7, 0))
                else:
                    above = field[p, r, z + 1, pl.ds(8 * xt + 1, 8), :]
                edge = edges if index == 0 else pltpu.roll(edges, 128 - 2 * index, 1)
                left = jnp.where(first_lane, edge, pltpu.roll(here, 1, 1))
                far = jnp.where(last_lane, edge, pltpu.roll(here, 127, 1))
                beside = ((z_lo + z_hi) + (below + above)) + (left + far)
                weight = diag[z, rows(xt), :]
                if p == 0:
                    value = right[r, z, rows(xt), :] - ((6.0 + weight) * here - beside)
                else:
                    value = ((weight + (6.0 - shift_value)) * here - beside) * (1.0 / scale_value)
                if p < POWERS - 1:
                    field[p + 1, r, z + 1, rows(xt), :] = value
                    packed = pack(packed, value, index)
                    keep_x_faces(p + 1, r, z, xt, value)
                else:
                    last[r, z, rows(xt), :] = value
        if p < POWERS - 1:
            y_send[p + 1, r] = packed
            for copy in halo_copies(p + 1, r):
                copy.start()

    def vector(p, r, z, xt):
        if p < POWERS - 1:
            return field[p + 1, r, z + 1, rows(xt), :]
        return last[r, z, rows(xt), :]

    def moments(p):
        n = len(PAIRS) * (1 if p == 0 else 2)

        def body(z, sums):
            sums = list(sums)
            for xt in range(xtiles):
                now = [vector(p, r, z, xt) for r in range(RHS)]
                products = []
                if p > 0:
                    before = [vector(p - 1, r, z, xt) for r in range(RHS)]
                    products += [before[r] * now[s] for r, s in PAIRS]
                products += [now[r] * now[s] for r, s in PAIRS]
                sums = [a + b for a, b in zip(sums, products, strict=True)]
            return tuple(sums)

        return list(lax.fori_loop(0, zlen, body, (jnp.zeros((8, 128), F32),) * n))

    def fold(sums, first_group):
        tile = jnp.zeros((8, 128), F32)
        for g in range(0, len(sums), 8):
            some = [jnp.sum(s, axis=0, keepdims=True) for s in sums[g : g + 8]]
            some += [jnp.zeros((1, 128), F32)] * (8 - len(some))
            sums_of = jnp.sum(jnp.concatenate(some, 0), axis=1, keepdims=True)
            tile = jnp.where(lane == first_group + g // 8, sums_of, tile)
        return tile

    out_copies = []
    early = []
    for p in range(POWERS):
        lax.fori_loop(0, RHS, lambda r, c, p=p: (step(p, r), c)[1], 0)
        if p < POWERS - 1:
            early += moments(p)
        else:
            late = moments(p)
        for r in range(RHS):
            src = field.at[p + 1, r, pl.ds(1, zlen)] if p < POWERS - 1 else last.at[r]
            copy = pltpu.make_async_copy(src, basis_hbm.at[p * RHS + r], out_sem.at[p * RHS + r])
            copy.start()
            out_copies.append(copy)
        if p == POWERS - 2:
            tile0[...] = fold(early, 0)

    tile0[...] += fold(late, EARLY_GROUPS)

    sends = []

    def exchange(src, dst, number, device):
        copy = pltpu.make_async_remote_copy(
            src_ref=src, dst_ref=dst, send_sem=sum_send.at[number],
            recv_sem=sum_recv.at[number], device_id=device, device_id_type=MESH,
        )
        copy.start()
        sends.append(copy)
        return copy

    mate = {"gy": gy + 1 - 2 * lax.rem(gy, 2)}
    exchange(tile0, pair_buf, 0, mate).wait_recv()
    tile1[...] = tile0[...] + pair_buf[...]

    slot = (gy // 2) * n_gz + gz
    copies = [
        exchange(tile1, plane_buf.at[slot], 1 + i, plane_dev(k)) for i, k in enumerate(plane)
    ]
    plane_buf[slot] = tile1[...]
    for copy in copies:
        copy.wait_recv()
    tile2[...] = tree_sum([plane_buf[i] for i in range(n_y * n_gz)])

    base = n_y * n_gz
    copies = [
        exchange(tile2, line_buf.at[gx], base + i, {"gx": ring("gx", k)})
        for i, k in enumerate(line)
    ]
    line_buf[gx] = tile2[...]
    for copy in copies:
        copy.wait_recv()
    total_out[...] = tree_sum([line_buf[i] for i in range(n_gx)])

    for copy in sends:
        copy.wait_send()
    for p in range(POWERS):
        for r in range(RHS):
            for copy in halo_copies(p, r):
                copy.wait_send()
    for copy in out_copies:
        copy.wait()


def factor_kernel(total, basis_hbm, ortho_hbm, factor, table, coeff, block, result, in_sem, out_sem):
    width = RHS * POWERS
    zlen, xlen = block.shape[1], block.shape[2]
    loads = [
        pltpu.make_async_copy(basis_hbm.at[:, z], block.at[:, z], in_sem.at[z]) for z in range(zlen)
    ]
    for copy in loads:
        copy.start()
    whole = total[...]
    for g in range(GROUPS):
        table[8 * g : 8 * g + 8, :] = jnp.broadcast_to(whole[:, g : g + 1], (8, 128))

    def gram(i, j):
        r, s = sorted((i % RHS, j % RHS))
        row = ROW_OF[(i // RHS + j // RHS, (r, s))]
        return jnp.broadcast_to(table[row : row + 1, :], (8, 128))

    lane = lax.broadcasted_iota(jnp.int32, (1, 128), 1)
    upper = {}
    for k in range(width):
        rest = {}
        for j in range(k, width):
            value = gram(k, j)
            for i in range(k):
                value = value - upper[i, k] * upper[i, j]
            rest[j] = value
        pivot = rest[k]
        inverse = lax.rsqrt(pivot)
        inverse = inverse * (1.5 - 0.5 * pivot * inverse * inverse)
        row = jnp.zeros((1, 128), F32)
        for j in range(k, width):
            upper[k, j] = rest[j] * inverse
            row = jnp.where(lane == j, upper[k, j][0:1, :], row)
            coeff[k * width + j] = inverse if j == k else upper[k, j]
        factor[k : k + 1, :] = row[:, :width]

    def body(z, carry):
        for xt in range(0, xlen // 8, 2):
            cols = [
                [block[j, z, pl.ds(8 * (xt + h), 8), :] for j in range(width)] for h in range(2)
            ]
            for i in range(width):
                scale = coeff[i * width + i]
                for h in range(2):
                    cols[h][i] = cols[h][i] * scale
                    result[i, z, pl.ds(8 * (xt + h), 8), :] = cols[h][i]
                for j in range(i + 1, width):
                    weight = coeff[i * width + j]
                    for h in range(2):
                        cols[h][j] = cols[h][j] - weight * cols[h][i]
        pltpu.make_async_copy(result.at[:, z], ortho_hbm.at[:, z], out_sem.at[z]).start()
        return carry

    for copy in loads:
        copy.wait()
    lax.fori_loop(0, zlen, body, 0)
    for z in range(zlen):
        pltpu.make_async_copy(result.at[:, z], ortho_hbm.at[:, z], out_sem.at[z]).wait()


def local(sizes, right_side, start_guess, diagonal):
    zlen, xlen, ylen = diagonal.shape
    width = RHS * POWERS
    block = (width, zlen, xlen, ylen)
    any_spec = pl.BlockSpec(memory_space=pl.ANY)
    vmem_spec = pl.BlockSpec(memory_space=pltpu.VMEM)
    n_gx, n_gy, n_gz = sizes
    planes = (n_gy // 2) * n_gz
    n_sum = planes + n_gx
    face = (POWERS, RHS, 8, 128)
    tile = pltpu.VMEM((8, 128), F32)
    basis, total = pl.pallas_call(
        functools.partial(power_kernel, sizes),
        out_shape=(jax.ShapeDtypeStruct(block, F32), jax.ShapeDtypeStruct((8, 128), F32)),
        in_specs=[any_spec] * 3,
        out_specs=(any_spec, vmem_spec),
        scratch_shapes=[
            pltpu.VMEM((POWERS, RHS, zlen + 2, xlen, ylen), F32),
            pltpu.VMEM((RHS, zlen, xlen, ylen), F32),
            pltpu.VMEM((RHS, zlen, xlen, ylen), F32),
            pltpu.VMEM((zlen, xlen, ylen), F32),
            pltpu.VMEM(face, F32),
            pltpu.VMEM(face, F32),
            pltpu.VMEM(face, F32),
            pltpu.VMEM((POWERS, RHS, 2, 8, 128), F32),
            pltpu.VMEM(face, F32),
            pltpu.VMEM(face, F32),
            tile,
            tile,
            tile,
            tile,
            pltpu.VMEM((planes, 8, 128), F32),
            pltpu.VMEM((n_gx, 8, 128), F32),
            pltpu.SemaphoreType.DMA((RHS + 2,)),
            pltpu.SemaphoreType.DMA((width,)),
            pltpu.SemaphoreType.DMA((POWERS, RHS, 6)),
            pltpu.SemaphoreType.DMA((POWERS, RHS, 6)),
            pltpu.SemaphoreType.DMA((n_sum,)),
            pltpu.SemaphoreType.DMA((n_sum,)),
        ],
        compiler_params=pltpu.CompilerParams(
            collective_id=0, has_side_effects=True, vmem_limit_bytes=24 << 20
        ),
    )(right_side, start_guess, diagonal)
    return pl.pallas_call(
        factor_kernel,
        out_shape=(
            jax.ShapeDtypeStruct(block, F32),
            jax.ShapeDtypeStruct((width, width), F32),
        ),
        in_specs=[vmem_spec, any_spec],
        out_specs=(any_spec, vmem_spec),
        scratch_shapes=[
            pltpu.VMEM((8 * GROUPS, 128), F32),
            pltpu.VMEM((width * width, 8, 128), F32),
            pltpu.VMEM(block, F32),
            pltpu.VMEM(block, F32),
            pltpu.SemaphoreType.DMA((zlen,)),
            pltpu.SemaphoreType.DMA((zlen,)),
        ],
        compiler_params=pltpu.CompilerParams(vmem_limit_bytes=24 << 20),
    )(total, basis)


def solution(mesh):
    placed = (P(None, "gz", "gx", "gy"), P(None, "gz", "gx", "gy"), P("gz", "gx", "gy"))
    sizes = tuple(mesh.shape[a] for a in ("gx", "gy", "gz"))
    return jax.shard_map(
        functools.partial(local, sizes),
        mesh=mesh,
        in_specs=placed,
        out_specs=(P(None, "gz", "gx", "gy"), P()),
        check_vma=False,
    )
```

time: 305 us -> 55.8 us (0.18)
  blocking collectives: 107 us -> 0 us
  starting transfers between devices: 72.6 us -> 0 us
  Pallas kernels: 0 us -> 52 us
  local copies, waits for them, and re-layouts: 42.3 us -> 2.98 us
  waiting for transfers between devices: 32.3 us -> 0 us
  matrix products: 19 us -> 0 us
  other arithmetic: 18.7 us -> 0 us
  between operations: 12.4 us -> 0.65 us
    psum x1 -> x0, blocking collectives: 107 us -> none  [local(): gram = lax.psum(local_gram, ('gx', 'gy', 'gz'))]
    ppermute x24 -> x0, starting transfers between devices: 72.6 us -> none  [the longest x12 53.4 us: with_halo(): lax.ppermute(lax.slice_in_dim(block, block.shape[dim] - width, None, axis...]
    pallas_call x0 -> x2, Pallas kernels: none -> 52 us  [the longest x1 48.7 us: local(): pl.pallas_call(functools.partial(power_kernel, sizes), out_shape=(jax.Sha...]
    ppermute x24 -> x0, waiting for transfers between devices: 32.3 us -> none  [the longest x12 26 us: with_halo(): lax.ppermute(lax.slice_in_dim(block, 0, width, axis=dim), axis, backward)]
    slice x62 -> x0, local copies, waits for them, and re-layouts: 25.8 us -> none  [the longest x16 9.45 us: upper_factor(): pivot = jnp.sqrt(rest[index])]
    dot_general x30 -> x0, matrix products: 19 us -> none  [the longest x14 11.5 us: upper_inverse(): jnp.dot(upper[index, index + 1:], later, precision=lax.Precision.HIGHEST)]
    div x5 -> x0, other arithmetic: 10.9 us -> none  [the longest x3 8.7 us: local(): vector = (apply_once(vector, diagonal) - shift_value * vector) / scale_value]
    unnamed x12 -> x6, local copies, waits for them, and re-layouts: 7.18 us -> 2.98 us
  transfers between devices with their start and end apart: 24 -> 0, of which waited for: 16 -> 0; matrix products, arithmetic and copies ran while one was open for 1% -> 0% of each run, Pallas kernels for 0% -> 0%
where the time goes in v1:
time: 55.8 us; the launch traced here: 55.6 us
  Pallas kernels  52 us (93%)
  local copies, waits for them, and re-layouts  2.98 us (5%)
  between operations  0.65 us (1%)
    pallas_call x1, Pallas kernels, local(): pl.pallas_call(functools.partial(power_kernel, sizes), out_shape=(jax.Sha...  48.7 us
    pallas_call x1, Pallas kernels, local(): pl.pallas_call(factor_kernel, out_shape=(jax.ShapeDtypeStruct(block, F32)...  3.24 us
    unnamed x6, local copies, waits for them, and re-layouts  2.98 us

profile of v1, /device:TPU:1, one launch (start us, length us, event | category | flops | bytes accessed | tf_op | source)
XLA Modules:
  0.0 55.6 jit_solution(11314600122418703400)
XLA Ops:
  0.6 0.0 copy-start
  0.6 1.0 %copy-done = f32[4,8,32,128]{3,2,1,0:T(8,128)S(1)} copy-done((f32[4,8,32,128]{3,2,1,0:T(8,128)S(1)}, f32[4,8,32,128]{3,2,1,0:T(8,128)}, u32[]{:S(2)}) %copy-start) | copy-done | bytes 524312
  1.7 0.0 copy-start.1
  1.7 1.0 %copy-done.1 = f32[4,8,32,128]{3,2,1,0:T(8,128)S(1)} copy-done((f32[4,8,32,128]{3,2,1,0:T(8,128)S(1)}, f32[4,8,32,128]{3,2,1,0:T(8,128)}, u32[]{:S(2)}) %copy-start.1) | copy-done | bytes 524312
  2.7 0.0 copy-start.2
  2.7 0.9 %copy-done.2 = f32[8,32,128]{2,1,0:T(8,128)S(1)} copy-done((f32[8,32,128]{2,1,0:T(8,128)S(1)}, f32[8,32,128]{2,1,0:T(8,128)}, u32[]{:S(2)}) %copy-start.2) | copy-done | bytes 131096
  3.6 48.7 %shard_map.50 = (f32[16,8,32,128]{3,2,1,0:T(8,128)S(1)}, f32[8,128]{1,0:T(8,128)S(1)}) custom-call(f32[4,8,32,128]{3,2,1,0:T(8,128)S(1)} %copy-done, f32[4,8,32,128]{3,2,1,0:T(8,128)S(1)} %copy-done.1, f32[8,32,128]{2,1,0:T(8,128)S(1)} %copy-done.2), custom_call_target="tpu_custom_call" | custom-call | tf_op jit(solution)/shard_map/pallas_call | solution.py:352
  52.4 3.2 %shard_map.51 = (f32[16,8,32,128]{3,2,1,0:T(8,128)}, f32[16,16]{1,0:T(8,128)}) custom-call(f32[8,128]{1,0:T(8,128)S(1)} %get-tuple-element.4.total, f32[16,8,32,128]{3,2,1,0:T(8,128)S(1)} %get-tuple-element.5.basis_hbm), custom_call_target="tpu_custom_call" | custom-call | tf_op jit(solution)/shard_map/pallas_call | solution.py:385
Async XLA Ops:
  0.6 1.0 %copy-start = (f32[4,8,32,128]{3,2,1,0:T(8,128)S(1)}, f32[4,8,32,128]{3,2,1,0:T(8,128)}, u32[]{:S(2)}) copy-start(f32[4,8,32,128]{3,2,1,0:T(8,128)} %right_hbm.1) | copy-start | bytes 1572868
  1.7 1.0 %copy-start.1 = (f32[4,8,32,128]{3,2,1,0:T(8,128)S(1)}, f32[4,8,32,128]{3,2,1,0:T(8,128)}, u32[]{:S(2)}) copy-start(f32[4,8,32,128]{3,2,1,0:T(8,128)} %guess_hbm.1) | copy-start | bytes 1572868
  2.7 0.9 %copy-start.2 = (f32[8,32,128]{2,1,0:T(8,128)S(1)}, f32[8,32,128]{2,1,0:T(8,128)}, u32[]{:S(2)}) copy-start(f32[8,32,128]{2,1,0:T(8,128)} %diag_hbm.1) | copy-start | bytes 393220

commit v2 on v1

--- a/solution.py
+++ b/solution.py
@@ -44,10 +44,10 @@
 
 
 def power_kernel(
-    sizes, right_hbm, guess_hbm, diag_hbm, basis_hbm, total_out,
-    field, last, right, diag, y_send, y_low, y_high, x_send, x_low, x_high,
+    sizes, right_hbm, guess_hbm, diag_hbm, basis, total_out,
+    guess, right, diag, z_low, z_high, y_send, y_low, y_high, x_send, x_low, x_high,
     tile0, tile1, tile2, pair_buf, plane_buf, line_buf,
-    in_sem, out_sem, halo_send, halo_recv, sum_send, sum_recv,
+    in_sem, halo_send, halo_recv, sum_send, sum_recv, relay_near, relay_far,
 ):
     n_gx, n_gy, n_gz = sizes
     n_y = n_gy // 2
@@ -56,7 +56,7 @@
     gx, gy, gz = (lax.axis_index(a) for a in ("gx", "gy", "gz"))
 
     load_guess = [
-        pltpu.make_async_copy(guess_hbm.at[r], field.at[0, r, pl.ds(1, zlen)], in_sem.at[r])
+        pltpu.make_async_copy(guess_hbm.at[r], guess.at[r], in_sem.at[r])
         for r in range(RHS)
     ]
     load_rest = [
@@ -77,9 +77,7 @@
         return {"gy": ring("gy", 2 * k[0]), "gz": ring("gz", k[1])}
 
     barrier = pltpu.get_barrier_semaphore()
-    greeted = [{"gy": ring("gy", 1)}, {"gy": ring("gy", -1)}]
-    greeted += [plane_dev(k) for k in reversed(plane)]
-    greeted += [{"gx": ring("gx", k)} for k in reversed(line)]
+    greeted = [{a: ring(a, k)} for a in ("gz", "gx", "gy") for k in (1, -1)]
     for device in greeted:
         pl.semaphore_signal(barrier, inc=1, device_id=device, device_id_type=MESH)
 
@@ -96,13 +94,17 @@
     def rows(xt):
         return pl.ds(8 * xt, 8)
 
+    def source(p, r):
+        return (guess, r) if p == 0 else (basis, (p - 1) * RHS + r)
+
     def pack(packed, value, index):
         return jnp.where(lane_half == index, pltpu.roll(value, 2 * index + 1, 1), packed)
 
     def halo_copies(p, r):
+        ref, slot = source(p, r)
         sends = [
-            (field.at[p, r, zlen], field.at[p, r, 0], {"gz": ring("gz", 1)}),
-            (field.at[p, r, 1], field.at[p, r, zlen + 1], {"gz": ring("gz", -1)}),
+            (ref.at[slot, zlen - 1], z_low.at[p, r], {"gz": ring("gz", 1)}),
+            (ref.at[slot, 0], z_high.at[p, r], {"gz": ring("gz", -1)}),
             (x_send.at[p, r, 1], x_low.at[p, r], {"gx": ring("gx", 1)}),
             (x_send.at[p, r, 0], x_high.at[p, r], {"gx": ring("gx", -1)}),
             (y_send.at[p, r], y_low.at[p, r], {"gy": ring("gy", 1)}),
@@ -127,7 +129,7 @@
         packed = jnp.zeros((8, 128), F32)
         for z in range(zlen):
             for xt in range(xtiles):
-                value = field[0, r, z + 1, rows(xt), :]
+                value = guess[r, z, rows(xt), :]
                 packed = pack(packed, value, z * xtiles + xt)
                 keep_x_faces(0, r, z, xt, value)
         y_send[0, r] = packed
@@ -139,6 +141,7 @@
         copy.wait()
 
     def step(p, r):
+        ref, slot = source(p, r)
         for copy in halo_copies(p, r):
             copy.wait_recv()
         edges = jnp.where(
@@ -150,21 +153,23 @@
         for z in range(zlen):
             for xt in range(xtiles):
                 index = z * xtiles + xt
-                here = field[p, r, z + 1, rows(xt), :]
-                z_lo = field[p, r, z, rows(xt), :]
-                z_hi = field[p, r, z + 2, rows(xt), :]
+                here = ref[slot, z, rows(xt), :]
                 if z == 0:
-                    z_lo = z_lo * z_has[0]
+                    z_lo = z_low[p, r, rows(xt), :] * z_has[0]
+                else:
+                    z_lo = ref[slot, z - 1, rows(xt), :]
                 if z == zlen - 1:
-                    z_hi = z_hi * z_has[1]
+                    z_hi = z_high[p, r, rows(xt), :] * z_has[1]
+                else:
+                    z_hi = ref[slot, z + 1, rows(xt), :]
                 if xt == 0:
                     below = jnp.where(first_row, x_lo[z : z + 1, :], pltpu.roll(here, 1, 0))
                 else:
-                    below = field[p, r, z + 1, pl.ds(8 * xt - 1, 8), :]
+                    below = ref[slot, z, pl.ds(8 * xt - 1, 8), :]
                 if xt == xtiles - 1:
                     above = jnp.where(last_row, x_hi[z : z + 1, :], pltpu.roll(here, 7, 0))
                 else:
-                    above = field[p, r, z + 1, pl.ds(8 * xt + 1, 8), :]
+                    above = ref[slot, z, pl.ds(8 * xt + 1, 8), :]
                 edge = edges if index == 0 else pltpu.roll(edges, 128 - 2 * index, 1)
                 left = jnp.where(first_lane, edge, pltpu.roll(here, 1, 1))
                 far = jnp.where(last_lane, edge, pltpu.roll(here, 127, 1))
@@ -174,21 +179,17 @@
                     value = right[r, z, rows(xt), :] - ((6.0 + weight) * here - beside)
                 else:
                     value = ((weight + (6.0 - shift_value)) * here - beside) * (1.0 / scale_value)
+                basis[p * RHS + r, z, rows(xt), :] = value
                 if p < POWERS - 1:
-                    field[p + 1, r, z + 1, rows(xt), :] = value
                     packed = pack(packed, value, index)
                     keep_x_faces(p + 1, r, z, xt, value)
-                else:
-                    last[r, z, rows(xt), :] = value
         if p < POWERS - 1:
             y_send[p + 1, r] = packed
             for copy in halo_copies(p + 1, r):
                 copy.start()
 
     def vector(p, r, z, xt):
-        if p < POWERS - 1:
-            return field[p + 1, r, z + 1, rows(xt), :]
-        return last[r, z, rows(xt), :]
+        return basis[p * RHS + r, z, rows(xt), :]
 
     def moments(p):
         n = len(PAIRS) * (1 if p == 0 else 2)
@@ -216,19 +217,31 @@
             tile = jnp.where(lane == first_group + g // 8, sums_of, tile)
         return tile
 
-    out_copies = []
+    relayed = n_gx == 16 and n_gy == 8
+
+    def relay(sem, offsets):
+        if relayed:
+            for axis, k in offsets:
+                pl.semaphore_signal(sem, inc=1, device_id={axis: ring(axis, k)}, device_id_type=MESH)
+
+    near = [(axis, k) for axis in ("gx", "gy") for k in (2, -2)]
+    far = [("gx", k) for k in (4, -4)]
+
     early = []
     for p in range(POWERS):
-        lax.fori_loop(0, RHS, lambda r, c, p=p: (step(p, r), c)[1], 0)
+        step(p, 0)
+        if p == 0:
+            relay(relay_near, near)
+        if p == 1 and relayed:
+            pl.semaphore_wait(relay_near, len(near))
+            relay(relay_far, far)
+        if p == POWERS - 1 and relayed:
+            pl.semaphore_wait(relay_far, len(far))
+        lax.fori_loop(1, RHS, lambda r, c, p=p: (step(p, r), c)[1], 0)
         if p < POWERS - 1:
             early += moments(p)
         else:
             late = moments(p)
-        for r in range(RHS):
-            src = field.at[p + 1, r, pl.ds(1, zlen)] if p < POWERS - 1 else last.at[r]
-            copy = pltpu.make_async_copy(src, basis_hbm.at[p * RHS + r], out_sem.at[p * RHS + r])
-            copy.start()
-            out_copies.append(copy)
         if p == POWERS - 2:
             tile0[...] = fold(early, 0)
 
@@ -274,18 +287,11 @@
         for r in range(RHS):
             for copy in halo_copies(p, r):
                 copy.wait_send()
-    for copy in out_copies:
-        copy.wait()
-
-
-def factor_kernel(total, basis_hbm, ortho_hbm, factor, table, coeff, block, result, in_sem, out_sem):
+
+
+def factor_kernel(total, basis, ortho_hbm, factor, table, coeff, result, out_sem):
     width = RHS * POWERS
-    zlen, xlen = block.shape[1], block.shape[2]
-    loads = [
-        pltpu.make_async_copy(basis_hbm.at[:, z], block.at[:, z], in_sem.at[z]) for z in range(zlen)
-    ]
-    for copy in loads:
-        copy.start()
+    zlen, xlen = basis.shape[1], basis.shape[2]
     whole = total[...]
     for g in range(GROUPS):
         table[8 * g : 8 * g + 8, :] = jnp.broadcast_to(whole[:, g : g + 1], (8, 128))
@@ -317,7 +323,7 @@
     def body(z, carry):
         for xt in range(0, xlen // 8, 2):
             cols = [
-                [block[j, z, pl.ds(8 * (xt + h), 8), :] for j in range(width)] for h in range(2)
+                [basis[j, z, pl.ds(8 * (xt + h), 8), :] for j in range(width)] for h in range(2)
             ]
             for i in range(width):
                 scale = coeff[i * width + i]
@@ -331,8 +337,6 @@
         pltpu.make_async_copy(result.at[:, z], ortho_hbm.at[:, z], out_sem.at[z]).start()
         return carry
 
-    for copy in loads:
-        copy.wait()
     lax.fori_loop(0, zlen, body, 0)
     for z in range(zlen):
         pltpu.make_async_copy(result.at[:, z], ortho_hbm.at[:, z], out_sem.at[z]).wait()
@@ -353,12 +357,13 @@
         functools.partial(power_kernel, sizes),
         out_shape=(jax.ShapeDtypeStruct(block, F32), jax.ShapeDtypeStruct((8, 128), F32)),
         in_specs=[any_spec] * 3,
-        out_specs=(any_spec, vmem_spec),
+        out_specs=(vmem_spec, vmem_spec),
         scratch_shapes=[
-            pltpu.VMEM((POWERS, RHS, zlen + 2, xlen, ylen), F32),
             pltpu.VMEM((RHS, zlen, xlen, ylen), F32),
             pltpu.VMEM((RHS, zlen, xlen, ylen), F32),
             pltpu.VMEM((zlen, xlen, ylen), F32),
+            pltpu.VMEM((POWERS, RHS, xlen, ylen), F32),
+            pltpu.VMEM((POWERS, RHS, xlen, ylen), F32),
             pltpu.VMEM(face, F32),
             pltpu.VMEM(face, F32),
             pltpu.VMEM(face, F32),
@@ -372,30 +377,29 @@
             pltpu.VMEM((planes, 8, 128), F32),
             pltpu.VMEM((n_gx, 8, 128), F32),
             pltpu.SemaphoreType.DMA((RHS + 2,)),
-            pltpu.SemaphoreType.DMA((width,)),
             pltpu.SemaphoreType.DMA((POWERS, RHS, 6)),
             pltpu.SemaphoreType.DMA((POWERS, RHS, 6)),
             pltpu.SemaphoreType.DMA((n_sum,)),
             pltpu.SemaphoreType.DMA((n_sum,)),
+            pltpu.SemaphoreType.REGULAR,
+            pltpu.SemaphoreType.REGULAR,
         ],
         compiler_params=pltpu.CompilerParams(
             collective_id=0, has_side_effects=True, vmem_limit_bytes=24 << 20
         ),
-    )(right_side, start_guess, diagonal)
+    )(*[pltpu.with_memory_space_constraint(x, pltpu.HBM) for x in (right_side, start_guess, diagonal)])
     return pl.pallas_call(
         factor_kernel,
         out_shape=(
             jax.ShapeDtypeStruct(block, F32),
             jax.ShapeDtypeStruct((width, width), F32),
         ),
-        in_specs=[vmem_spec, any_spec],
+        in_specs=[vmem_spec, vmem_spec],
         out_specs=(any_spec, vmem_spec),
         scratch_shapes=[
             pltpu.VMEM((8 * GROUPS, 128), F32),
             pltpu.VMEM((width * width, 8, 128), F32),
             pltpu.VMEM(block, F32),
-            pltpu.VMEM(block, F32),
-            pltpu.SemaphoreType.DMA((zlen,)),
             pltpu.SemaphoreType.DMA((zlen,)),
         ],
         compiler_params=pltpu.CompilerParams(vmem_limit_bytes=24 << 20),

time: 55.8 us -> 47.5 us (0.85)
  Pallas kernels: 52 us -> 46.7 us
  local copies, waits for them, and re-layouts: 2.98 us -> 0 us
    pallas_call x1, Pallas kernels: 48.7 us -> 43.8 us  [local(): pl.pallas_call(functools.partial(power_kernel, sizes), out_shape=(jax.Sha...]
    unnamed x6 -> x0, local copies, waits for them, and re-layouts: 2.98 us -> none
where the time goes in v2:
time: 47.5 us; the launch traced here: 47.4 us
  Pallas kernels  46.7 us (98%)
  between operations  0.64 us (1%)
    pallas_call x1, Pallas kernels, local(): pl.pallas_call(functools.partial(power_kernel, sizes), out_shape=(jax.Sha...  43.8 us
    pallas_call x1, Pallas kernels, local(): pl.pallas_call(factor_kernel, out_shape=(jax.ShapeDtypeStruct(block, F32)...  2.96 us

profile of v2, /device:TPU:1, one launch (start us, length us, event | category | flops | bytes accessed | tf_op | source)
XLA Modules:
  0.0 47.4 jit_solution(16716892489231288082)
XLA Ops:
  0.6 43.8 %shard_map.50 = (f32[16,8,32,128]{3,2,1,0:T(8,128)S(1)}, f32[8,128]{1,0:T(8,128)S(1)}) custom-call(f32[4,8,32,128]{3,2,1,0:T(8,128)} %right_hbm.1, f32[4,8,32,128]{3,2,1,0:T(8,128)} %guess_hbm.1, f32[8,32,128]{2,1,0:T(8,128)} %diag_hbm.1), custom_call_target="tpu_custom_call" | custom-call | tf_op jit(solution)/shard_map/pallas_call | solution.py:356
  44.4 3.0 %shard_map.51 = (f32[16,8,32,128]{3,2,1,0:T(8,128)}, f32[16,16]{1,0:T(8,128)}) custom-call(f32[8,128]{1,0:T(8,128)S(1)} %get-tuple-element.4.total, f32[16,8,32,128]{3,2,1,0:T(8,128)S(1)} %get-tuple-element.5.basis), custom_call_target="tpu_custom_call" | custom-call | tf_op jit(solution)/shard_map/pallas_call | solution.py:391

commit v3 on v2

--- a/solution.py
+++ b/solution.py
@@ -46,7 +46,7 @@
 def power_kernel(
     sizes, right_hbm, guess_hbm, diag_hbm, basis, total_out,
     guess, right, diag, z_low, z_high, y_send, y_low, y_high, x_send, x_low, x_high,
-    tile0, tile1, tile2, pair_buf, plane_buf, line_buf,
+    tile0, tile1, tile2, pair_buf, plane_buf, line_buf, count_ref,
     in_sem, halo_send, halo_recv, sum_send, sum_recv, relay_near, relay_far,
 ):
     n_gx, n_gy, n_gz = sizes
@@ -100,7 +100,7 @@
     def pack(packed, value, index):
         return jnp.where(lane_half == index, pltpu.roll(value, 2 * index + 1, 1), packed)
 
-    def halo_copies(p, r):
+    def send_halos(p, r, part):
         ref, slot = source(p, r)
         sends = [
             (ref.at[slot, zlen - 1], z_low.at[p, r], {"gz": ring("gz", 1)}),
@@ -110,13 +110,17 @@
             (y_send.at[p, r], y_low.at[p, r], {"gy": ring("gy", 1)}),
             (y_send.at[p, r], y_high.at[p, r], {"gy": ring("gy", -1)}),
         ]
-        return [
+        for src, dst, device in sends[part]:
             pltpu.make_async_remote_copy(
-                src_ref=src, dst_ref=dst, send_sem=halo_send.at[p, r, i],
-                recv_sem=halo_recv.at[p, r, i], device_id=device, device_id_type=MESH,
-            )
-            for i, (src, dst, device) in enumerate(sends)
-        ]
+                src_ref=src, dst_ref=dst, send_sem=halo_send.at[p],
+                recv_sem=halo_recv.at[p, r], device_id=device, device_id_type=MESH,
+            ).start()
+
+    def wait_bytes(like, sem):
+        pltpu.make_async_copy(like, like, sem).wait()
+
+    def wait_halos(p, r):
+        wait_bytes(right_hbm.at[0, pl.ds(0, 3)], halo_recv.at[p, r])
 
     def keep_x_faces(p, r, z, xt, value):
         if xt == 0:
@@ -135,22 +139,22 @@
         y_send[0, r] = packed
         if r == 0:
             pl.semaphore_wait(barrier, len(greeted))
-        for copy in halo_copies(0, r):
-            copy.start()
+        send_halos(0, r, slice(0, 6))
     for copy in load_rest:
         copy.wait()
 
     def step(p, r):
         ref, slot = source(p, r)
-        for copy in halo_copies(p, r):
-            copy.wait_recv()
+        wait_halos(p, r)
         edges = jnp.where(
             odd, pltpu.roll(y_high[p, r] * y_has[1], 126, 1), y_low[p, r] * y_has[0]
         )
         x_lo = x_low[p, r] * x_has[0]
         x_hi = x_high[p, r] * x_has[1]
         packed = jnp.zeros((8, 128), F32)
-        for z in range(zlen):
+        for z in [0, zlen - 1, *range(1, zlen - 1)]:
+            if p < POWERS - 1 and z == 1:
+                send_halos(p + 1, r, slice(0, 2))
             for xt in range(xtiles):
                 index = z * xtiles + xt
                 here = ref[slot, z, rows(xt), :]
@@ -185,8 +189,7 @@
                     keep_x_faces(p + 1, r, z, xt, value)
         if p < POWERS - 1:
             y_send[p + 1, r] = packed
-            for copy in halo_copies(p + 1, r):
-                copy.start()
+            send_halos(p + 1, r, slice(2, 6))
 
     def vector(p, r, z, xt):
         return basis[p * RHS + r, z, rows(xt), :]
@@ -214,8 +217,8 @@
             some = [jnp.sum(s, axis=0, keepdims=True) for s in sums[g : g + 8]]
             some += [jnp.zeros((1, 128), F32)] * (8 - len(some))
             sums_of = jnp.sum(jnp.concatenate(some, 0), axis=1, keepdims=True)
-            tile = jnp.where(lane == first_group + g // 8, sums_of, tile)
-        return tile
+            tile = jnp.where(lane == 8 * first_group + g + sub, sums_of, tile)
+        return jnp.sum(tile, axis=0, keepdims=True)
 
     relayed = n_gx == 16 and n_gy == 8
 
@@ -247,54 +250,50 @@
 
     tile0[...] += fold(late, EARLY_GROUPS)
 
-    sends = []
-
-    def exchange(src, dst, number, device):
-        copy = pltpu.make_async_remote_copy(
-            src_ref=src, dst_ref=dst, send_sem=sum_send.at[number],
-            recv_sem=sum_recv.at[number], device_id=device, device_id_type=MESH,
-        )
-        copy.start()
-        sends.append(copy)
-        return copy
-
-    mate = {"gy": gy + 1 - 2 * lax.rem(gy, 2)}
-    exchange(tile0, pair_buf, 0, mate).wait_recv()
+    def exchange(src, dst, phase, device):
+        pltpu.make_async_remote_copy(
+            src_ref=src, dst_ref=dst, send_sem=sum_send.at[phase],
+            recv_sem=sum_recv.at[phase], device_id=device, device_id_type=MESH,
+        ).start()
+
+    def wait_sums(sems, phase, number):
+        wait_bytes(count_ref.at[pl.ds(0, number)], sems.at[phase])
+
+    n_plane = n_y * n_gz
+    slot = (gy // 2) * n_gz + gz
+
+    exchange(tile0, pair_buf, 0, {"gy": gy + 1 - 2 * lax.rem(gy, 2)})
+    wait_sums(sum_recv, 0, 1)
     tile1[...] = tile0[...] + pair_buf[...]
 
-    slot = (gy // 2) * n_gz + gz
-    copies = [
-        exchange(tile1, plane_buf.at[slot], 1 + i, plane_dev(k)) for i, k in enumerate(plane)
-    ]
+    for k in plane:
+        exchange(tile1, plane_buf.at[slot], 1, plane_dev(k))
     plane_buf[slot] = tile1[...]
-    for copy in copies:
-        copy.wait_recv()
-    tile2[...] = tree_sum([plane_buf[i] for i in range(n_y * n_gz)])
-
-    base = n_y * n_gz
-    copies = [
-        exchange(tile2, line_buf.at[gx], base + i, {"gx": ring("gx", k)})
-        for i, k in enumerate(line)
-    ]
+    for p in range(POWERS):
+        wait_bytes(right_hbm.at[:, pl.ds(0, 3)], halo_send.at[p])
+    wait_sums(sum_send, 0, 1)
+    wait_sums(sum_recv, 1, n_plane - 1)
+    tile2[...] = tree_sum([plane_buf[i] for i in range(n_plane)])
+
+    for k in line:
+        exchange(tile2, line_buf.at[gx], 2, {"gx": ring("gx", k)})
     line_buf[gx] = tile2[...]
-    for copy in copies:
-        copy.wait_recv()
+    wait_sums(sum_send, 1, n_plane - 1)
+    wait_sums(sum_recv, 2, n_gx - 1)
     total_out[...] = tree_sum([line_buf[i] for i in range(n_gx)])
-
-    for copy in sends:
-        copy.wait_send()
-    for p in range(POWERS):
-        for r in range(RHS):
-            for copy in halo_copies(p, r):
-                copy.wait_send()
+    wait_sums(sum_send, 2, n_gx - 1)
 
 
 def factor_kernel(total, basis, ortho_hbm, factor, table, coeff, result, out_sem):
     width = RHS * POWERS
     zlen, xlen = basis.shape[1], basis.shape[2]
     whole = total[...]
+    places = lax.broadcasted_iota(jnp.int32, (8, 128), 1) - lax.broadcasted_iota(
+        jnp.int32, (8, 128), 0
+    )
     for g in range(GROUPS):
-        table[8 * g : 8 * g + 8, :] = jnp.broadcast_to(whole[:, g : g + 1], (8, 128))
+        column = jnp.sum(jnp.where(places == 8 * g, whole, 0.0), axis=1, keepdims=True)
+        table[8 * g : 8 * g + 8, :] = jnp.broadcast_to(column, (8, 128))
 
     def gram(i, j):
         r, s = sorted((i % RHS, j % RHS))
@@ -350,12 +349,11 @@
     vmem_spec = pl.BlockSpec(memory_space=pltpu.VMEM)
     n_gx, n_gy, n_gz = sizes
     planes = (n_gy // 2) * n_gz
-    n_sum = planes + n_gx
     face = (POWERS, RHS, 8, 128)
-    tile = pltpu.VMEM((8, 128), F32)
+    tile = pltpu.VMEM((1, 128), F32)
     basis, total = pl.pallas_call(
         functools.partial(power_kernel, sizes),
-        out_shape=(jax.ShapeDtypeStruct(block, F32), jax.ShapeDtypeStruct((8, 128), F32)),
+        out_shape=(jax.ShapeDtypeStruct(block, F32), jax.ShapeDtypeStruct((1, 128), F32)),
         in_specs=[any_spec] * 3,
         out_specs=(vmem_spec, vmem_spec),
         scratch_shapes=[
@@ -374,13 +372,14 @@
             tile,
             tile,
             tile,
-            pltpu.VMEM((planes, 8, 128), F32),
-            pltpu.VMEM((n_gx, 8, 128), F32),
+            pltpu.VMEM((planes, 1, 128), F32),
+            pltpu.VMEM((n_gx, 1, 128), F32),
+            pltpu.VMEM((max(planes, n_gx), 1, 128), F32),
             pltpu.SemaphoreType.DMA((RHS + 2,)),
-            pltpu.SemaphoreType.DMA((POWERS, RHS, 6)),
-            pltpu.SemaphoreType.DMA((POWERS, RHS, 6)),
-            pltpu.SemaphoreType.DMA((n_sum,)),
-            pltpu.SemaphoreType.DMA((n_sum,)),
+            pltpu.SemaphoreType.DMA((POWERS,)),
+            pltpu.SemaphoreType.DMA((POWERS, RHS)),
+            pltpu.SemaphoreType.DMA((3,)),
+            pltpu.SemaphoreType.DMA((3,)),
             pltpu.SemaphoreType.REGULAR,
             pltpu.SemaphoreType.REGULAR,
         ],

time: 47.5 us -> 44.5 us (0.937)
  Pallas kernels: 46.7 us -> 43.8 us
    pallas_call x1, Pallas kernels: 43.8 us -> 40.8 us  [local(): pl.pallas_call(functools.partial(power_kernel, sizes), out_shape=(jax.Sha...]
where the time goes in v3:
time: 44.5 us; the launch traced here: 44.4 us
  Pallas kernels  43.8 us (98%)
  between operations  0.64 us (1%)
    pallas_call x1, Pallas kernels, local(): pl.pallas_call(functools.partial(power_kernel, sizes), out_shape=(jax.Sha...  40.8 us
    pallas_call x1, Pallas kernels, local(): pl.pallas_call(factor_kernel, out_shape=(jax.ShapeDtypeStruct(block, F32)...  2.96 us

profile of v3, /device:TPU:1, one launch (start us, length us, event | category | flops | bytes accessed | tf_op | source)
XLA Modules:
  0.0 44.4 jit_solution(17098185773694623676)
XLA Ops:
  0.6 40.8 %shard_map.50 = (f32[16,8,32,128]{3,2,1,0:T(8,128)S(1)}, f32[1,128]{1,0:T(1,128)S(1)}) custom-call(f32[4,8,32,128]{3,2,1,0:T(8,128)} %right_hbm.1, f32[4,8,32,128]{3,2,1,0:T(8,128)} %guess_hbm.1, f32[8,32,128]{2,1,0:T(8,128)} %diag_hbm.1), custom_call_target="tpu_custom_call" | custom-call | tf_op jit(solution)/shard_map/pallas_call | solution.py:354
  41.4 3.0 %shard_map.51 = (f32[16,8,32,128]{3,2,1,0:T(8,128)}, f32[16,16]{1,0:T(8,128)}) custom-call(f32[1,128]{1,0:T(1,128)S(1)} %get-tuple-element.4.total, f32[16,8,32,128]{3,2,1,0:T(8,128)S(1)} %get-tuple-element.5.basis), custom_call_target="tpu_custom_call" | custom-call | tf_op jit(solution)/shard_map/pallas_call | solution.py:390

commit v4 on v3

--- a/solution.py
+++ b/solution.py
@@ -16,12 +16,17 @@
 
 PAIRS = [(r, s) for r in range(RHS) for s in range(r, RHS)]
 EARLY = [(k, pair) for k in range(5) for pair in PAIRS]
-LATE = [(k, pair) for k in (5, 6) for pair in PAIRS]
-EARLY_GROUPS = -(-len(EARLY) // 8)
-LATE_GROUPS = -(-len(LATE) // 8)
-GROUPS = EARLY_GROUPS + LATE_GROUPS
-ROW_OF = {entry: row for row, entry in enumerate(EARLY)}
-ROW_OF.update({entry: EARLY_GROUPS * 8 + row for row, entry in enumerate(LATE)})
+LATE = [[(k, (r, s)) for k in (5, 6) for r in range(s + 1)] for s in range(RHS)]
+BATCHES = [EARLY, sum(LATE[:-1], []), LATE[-1]]
+FIRST_GROUP = [0]
+for entries in BATCHES:
+    FIRST_GROUP.append(FIRST_GROUP[-1] - (-len(entries) // 8))
+GROUPS = FIRST_GROUP[-1]
+ROW_OF = {
+    entry: 8 * first + row
+    for first, entries in zip(FIRST_GROUP, BATCHES)
+    for row, entry in enumerate(entries)
+}
 
 
 def ring(axis, offset):
@@ -56,15 +61,13 @@
     gx, gy, gz = (lax.axis_index(a) for a in ("gx", "gy", "gz"))
 
     load_guess = [
-        pltpu.make_async_copy(guess_hbm.at[r], guess.at[r], in_sem.at[r])
-        for r in range(RHS)
+        pltpu.make_async_copy(guess_hbm.at[r], guess.at[r], in_sem.at[r]) for r in range(RHS)
     ]
     load_rest = [
         pltpu.make_async_copy(diag_hbm, diag, in_sem.at[RHS]),
         pltpu.make_async_copy(right_hbm, right, in_sem.at[RHS + 1]),
     ]
-    for copy in load_guess + load_rest:
-        copy.start()
+    load_guess[0].start()
 
     def dist(k, n):
         return min(k, n - k)
@@ -80,6 +83,9 @@
     greeted = [{a: ring(a, k)} for a in ("gz", "gx", "gy") for k in (1, -1)]
     for device in greeted:
         pl.semaphore_signal(barrier, inc=1, device_id=device, device_id_type=MESH)
+
+    for copy in load_guess[1:] + load_rest:
+        copy.start()
 
     lane = lax.broadcasted_iota(jnp.int32, (8, 128), 1)
     sub = lax.broadcasted_iota(jnp.int32, (8, 128), 0)
@@ -145,6 +151,7 @@
 
     def step(p, r):
         ref, slot = source(p, r)
+        sums = [jnp.zeros((8, 128), F32)] * (2 * (r + 1) if p == POWERS - 1 else 0)
         wait_halos(p, r)
         edges = jnp.where(
             odd, pltpu.roll(y_high[p, r] * y_has[1], 126, 1), y_low[p, r] * y_has[0]
@@ -184,12 +191,17 @@
                 else:
                     value = ((weight + (6.0 - shift_value)) * here - beside) * (1.0 / scale_value)
                 basis[p * RHS + r, z, rows(xt), :] = value
+                if p == POWERS - 1:
+                    others = [basis[(p - 1) * RHS + q, z, rows(xt), :] for q in range(r)] + [here]
+                    others += [basis[p * RHS + q, z, rows(xt), :] for q in range(r)] + [value]
+                    sums = [a + b * value for a, b in zip(sums, others, strict=True)]
                 if p < POWERS - 1:
                     packed = pack(packed, value, index)
                     keep_x_faces(p + 1, r, z, xt, value)
         if p < POWERS - 1:
             y_send[p + 1, r] = packed
             send_halos(p + 1, r, slice(2, 6))
+        return sums
 
     def vector(p, r, z, xt):
         return basis[p * RHS + r, z, rows(xt), :]
@@ -231,24 +243,25 @@
     far = [("gx", k) for k in (4, -4)]
 
     early = []
-    for p in range(POWERS):
+    for p in range(POWERS - 1):
         step(p, 0)
         if p == 0:
             relay(relay_near, near)
         if p == 1 and relayed:
             pl.semaphore_wait(relay_near, len(near))
             relay(relay_far, far)
-        if p == POWERS - 1 and relayed:
-            pl.semaphore_wait(relay_far, len(far))
         lax.fori_loop(1, RHS, lambda r, c, p=p: (step(p, r), c)[1], 0)
-        if p < POWERS - 1:
-            early += moments(p)
-        else:
-            late = moments(p)
-        if p == POWERS - 2:
-            tile0[...] = fold(early, 0)
-
-    tile0[...] += fold(late, EARLY_GROUPS)
+        early += moments(p)
+    tile0[...] = fold(early, FIRST_GROUP[0])
+
+    late = []
+    for r in range(RHS - 1):
+        late += step(POWERS - 1, r)
+    tile0[...] += fold(late, FIRST_GROUP[1])
+    if relayed:
+        pl.semaphore_wait(relay_far, len(far))
+    late = step(POWERS - 1, RHS - 1)
+    tile0[...] += fold(late, FIRST_GROUP[2])
 
     def exchange(src, dst, phase, device):
         pltpu.make_async_remote_copy(
@@ -284,7 +297,9 @@
     wait_sums(sum_send, 2, n_gx - 1)
 
 
-def factor_kernel(total, basis, ortho_hbm, factor, table, coeff, result, out_sem):
+def factor_kernel(
+    total, basis, ortho_hbm, factor_hbm, table, coeff, result, factor, out_sem, factor_sem
+):
     width = RHS * POWERS
     zlen, xlen = basis.shape[1], basis.shape[2]
     whole = total[...]
@@ -318,6 +333,8 @@
             row = jnp.where(lane == j, upper[k, j][0:1, :], row)
             coeff[k * width + j] = inverse if j == k else upper[k, j]
         factor[k : k + 1, :] = row[:, :width]
+    factor_copy = pltpu.make_async_copy(factor, factor_hbm, factor_sem)
+    factor_copy.start()
 
     def body(z, carry):
         for xt in range(0, xlen // 8, 2):
@@ -339,6 +356,7 @@
     lax.fori_loop(0, zlen, body, 0)
     for z in range(zlen):
         pltpu.make_async_copy(result.at[:, z], ortho_hbm.at[:, z], out_sem.at[z]).wait()
+    factor_copy.wait()
 
 
 def local(sizes, right_side, start_guess, diagonal):
@@ -394,12 +412,14 @@
             jax.ShapeDtypeStruct((width, width), F32),
         ),
         in_specs=[vmem_spec, vmem_spec],
-        out_specs=(any_spec, vmem_spec),
+        out_specs=(any_spec, any_spec),
         scratch_shapes=[
             pltpu.VMEM((8 * GROUPS, 128), F32),
             pltpu.VMEM((width * width, 8, 128), F32),
             pltpu.VMEM(block, F32),
+            pltpu.VMEM((width, width), F32),
             pltpu.SemaphoreType.DMA((zlen,)),
+            pltpu.SemaphoreType.DMA,
         ],
         compiler_params=pltpu.CompilerParams(vmem_limit_bytes=24 << 20),
     )(total, basis)

time: 44.5 us -> 43.7 us (0.982)
  Pallas kernels: 43.8 us -> 43 us
    pallas_call x1, Pallas kernels: 2.96 us -> 2.38 us  [local(): pl.pallas_call(factor_kernel, out_shape=(jax.ShapeDtypeStruct(block, F32)...]
where the time goes in v4:
time: 43.7 us; the launch traced here: 43.6 us
  Pallas kernels  43 us (98%)
  between operations  0.64 us (1%)
    pallas_call x1, Pallas kernels, local(): pl.pallas_call(functools.partial(power_kernel, sizes), out_shape=(jax.Sha...  40.6 us
    pallas_call x1, Pallas kernels, local(): pl.pallas_call(factor_kernel, out_shape=(jax.ShapeDtypeStruct(block, F32)...  2.38 us

profile of v4, /device:TPU:1, one launch (start us, length us, event | category | flops | bytes accessed | tf_op | source)
XLA Modules:
  0.0 43.6 jit_solution(9028796061657556022)
XLA Ops:
  0.6 40.6 %shard_map.50 = (f32[16,8,32,128]{3,2,1,0:T(8,128)S(1)}, f32[1,128]{1,0:T(1,128)S(1)}) custom-call(f32[4,8,32,128]{3,2,1,0:T(8,128)} %right_hbm.1, f32[4,8,32,128]{3,2,1,0:T(8,128)} %guess_hbm.1, f32[8,32,128]{2,1,0:T(8,128)} %diag_hbm.1), custom_call_target="tpu_custom_call" | custom-call | tf_op jit(solution)/shard_map/pallas_call | solution.py:372
  41.2 2.4 %shard_map.51 = (f32[16,8,32,128]{3,2,1,0:T(8,128)}, f32[16,16]{1,0:T(8,128)}) custom-call(f32[1,128]{1,0:T(1,128)S(1)} %get-tuple-element.4.total, f32[16,8,32,128]{3,2,1,0:T(8,128)S(1)} %get-tuple-element.5.basis), custom_call_target="tpu_custom_call" | custom-call | tf_op jit(solution)/shard_map/pallas_call | solution.py:408

commit v5 on v4

--- a/solution.py
+++ b/solution.py
@@ -50,7 +50,7 @@
 
 def power_kernel(
     sizes, right_hbm, guess_hbm, diag_hbm, basis, total_out,
-    guess, right, diag, z_low, z_high, y_send, y_low, y_high, x_send, x_low, x_high,
+    guess, right, diag, partial, z_low, z_high, y_send, y_low, y_high, x_send, x_low, x_high,
     tile0, tile1, tile2, pair_buf, plane_buf, line_buf, count_ref,
     in_sem, halo_send, halo_recv, sum_send, sum_recv, relay_near, relay_far,
 ):
@@ -149,58 +149,82 @@
     for copy in load_rest:
         copy.wait()
 
-    def step(p, r):
+    both_lanes = first_lane | last_lane
+
+    def inside(p, r, carry):
         ref, slot = source(p, r)
-        sums = [jnp.zeros((8, 128), F32)] * (2 * (r + 1) if p == POWERS - 1 else 0)
-        wait_halos(p, r)
-        edges = jnp.where(
-            odd, pltpu.roll(y_high[p, r] * y_has[1], 126, 1), y_low[p, r] * y_has[0]
-        )
-        x_lo = x_low[p, r] * x_has[0]
-        x_hi = x_high[p, r] * x_has[1]
-        packed = jnp.zeros((8, 128), F32)
-        for z in [0, zlen - 1, *range(1, zlen - 1)]:
-            if p < POWERS - 1 and z == 1:
-                send_halos(p + 1, r, slice(0, 2))
+        for z in range(zlen):
             for xt in range(xtiles):
-                index = z * xtiles + xt
                 here = ref[slot, z, rows(xt), :]
-                if z == 0:
-                    z_lo = z_low[p, r, rows(xt), :] * z_has[0]
-                else:
-                    z_lo = ref[slot, z - 1, rows(xt), :]
-                if z == zlen - 1:
-                    z_hi = z_high[p, r, rows(xt), :] * z_has[1]
-                else:
-                    z_hi = ref[slot, z + 1, rows(xt), :]
                 if xt == 0:
-                    below = jnp.where(first_row, x_lo[z : z + 1, :], pltpu.roll(here, 1, 0))
+                    below = jnp.where(first_row, 0.0, pltpu.roll(here, 1, 0))
                 else:
                     below = ref[slot, z, pl.ds(8 * xt - 1, 8), :]
                 if xt == xtiles - 1:
-                    above = jnp.where(last_row, x_hi[z : z + 1, :], pltpu.roll(here, 7, 0))
+                    above = jnp.where(last_row, 0.0, pltpu.roll(here, 7, 0))
                 else:
                     above = ref[slot, z, pl.ds(8 * xt + 1, 8), :]
-                edge = edges if index == 0 else pltpu.roll(edges, 128 - 2 * index, 1)
-                left = jnp.where(first_lane, edge, pltpu.roll(here, 1, 1))
-                far = jnp.where(last_lane, edge, pltpu.roll(here, 127, 1))
-                beside = ((z_lo + z_hi) + (below + above)) + (left + far)
+                left = jnp.where(first_lane, 0.0, pltpu.roll(here, 1, 1))
+                other = jnp.where(last_lane, 0.0, pltpu.roll(here, 127, 1))
+                beside = (below + above) + (left + other)
+                if z > 0:
+                    beside = beside + ref[slot, z - 1, rows(xt), :]
+                if z < zlen - 1:
+                    beside = beside + ref[slot, z + 1, rows(xt), :]
                 weight = diag[z, rows(xt), :]
                 if p == 0:
                     value = right[r, z, rows(xt), :] - ((6.0 + weight) * here - beside)
                 else:
                     value = ((weight + (6.0 - shift_value)) * here - beside) * (1.0 / scale_value)
-                basis[p * RHS + r, z, rows(xt), :] = value
-                if p == POWERS - 1:
-                    others = [basis[(p - 1) * RHS + q, z, rows(xt), :] for q in range(r)] + [here]
-                    others += [basis[p * RHS + q, z, rows(xt), :] for q in range(r)] + [value]
-                    sums = [a + b * value for a, b in zip(sums, others, strict=True)]
-                if p < POWERS - 1:
-                    packed = pack(packed, value, index)
-                    keep_x_faces(p + 1, r, z, xt, value)
+                partial[r, z, rows(xt), :] = value
+        return carry
+
+    z_ends = (0, zlen - 1)
+    x_ends = (0, xtiles - 1)
+    order = [(z, xt) for z in z_ends for xt in range(xtiles)]
+    order += [(z, xt) for z in range(1, zlen - 1) for xt in x_ends]
+    x_done = len(order)
+    order += [(z, xt) for z in range(1, zlen - 1) for xt in range(1, xtiles - 1)]
+
+    def step(p, r):
+        sums = [jnp.zeros((8, 128), F32)] * (2 * (r + 1) if p == POWERS - 1 else 0)
+        sign = 1.0 if p == 0 else -1.0 / scale_value
+        wait_halos(p, r)
+        edges = jnp.where(
+            odd,
+            pltpu.roll(y_high[p, r] * (y_has[1] * sign), 126, 1),
+            y_low[p, r] * (y_has[0] * sign),
+        )
+        x_lo = x_low[p, r] * (x_has[0] * sign)
+        x_hi = x_high[p, r] * (x_has[1] * sign)
+        packed = jnp.zeros((8, 128), F32)
+        for count, (z, xt) in enumerate(order):
+            index = z * xtiles + xt
+            edge = edges if index == 0 else pltpu.roll(edges, 128 - 2 * index, 1)
+            value = partial[r, z, rows(xt), :] + jnp.where(both_lanes, edge, 0.0)
+            if z == 0:
+                value = value + z_low[p, r, rows(xt), :] * (z_has[0] * sign)
+            if z == zlen - 1:
+                value = value + z_high[p, r, rows(xt), :] * (z_has[1] * sign)
+            if xt == 0:
+                value = value + jnp.where(first_row, x_lo[z : z + 1, :], 0.0)
+            if xt == xtiles - 1:
+                value = value + jnp.where(last_row, x_hi[z : z + 1, :], 0.0)
+            basis[p * RHS + r, z, rows(xt), :] = value
+            if p == POWERS - 1:
+                others = [basis[(p - 1) * RHS + q, z, rows(xt), :] for q in range(r + 1)]
+                others += [basis[p * RHS + q, z, rows(xt), :] for q in range(r)] + [value]
+                sums = [a + b * value for a, b in zip(sums, others, strict=True)]
+            else:
+                packed = pack(packed, value, index)
+                keep_x_faces(p + 1, r, z, xt, value)
+                if count + 1 == 2 * xtiles:
+                    send_halos(p + 1, r, slice(0, 2))
+                if count + 1 == x_done:
+                    send_halos(p + 1, r, slice(2, 4))
         if p < POWERS - 1:
             y_send[p + 1, r] = packed
-            send_halos(p + 1, r, slice(2, 6))
+            send_halos(p + 1, r, slice(4, 6))
         return sums
 
     def vector(p, r, z, xt):
@@ -244,6 +268,9 @@
 
     early = []
     for p in range(POWERS - 1):
+        lax.fori_loop(0, RHS, functools.partial(inside, p), 0)
+        if p > 0:
+            early += moments(p - 1)
         step(p, 0)
         if p == 0:
             relay(relay_near, near)
@@ -251,7 +278,8 @@
             pl.semaphore_wait(relay_near, len(near))
             relay(relay_far, far)
         lax.fori_loop(1, RHS, lambda r, c, p=p: (step(p, r), c)[1], 0)
-        early += moments(p)
+    lax.fori_loop(0, RHS, functools.partial(inside, POWERS - 1), 0)
+    early += moments(POWERS - 2)
     tile0[...] = fold(early, FIRST_GROUP[0])
 
     late = []
@@ -378,6 +406,7 @@
             pltpu.VMEM((RHS, zlen, xlen, ylen), F32),
             pltpu.VMEM((RHS, zlen, xlen, ylen), F32),
             pltpu.VMEM((zlen, xlen, ylen), F32),
+            pltpu.VMEM((RHS, zlen, xlen, ylen), F32),
             pltpu.VMEM((POWERS, RHS, xlen, ylen), F32),
             pltpu.VMEM((POWERS, RHS, xlen, ylen), F32),
             pltpu.VMEM(face, F32),

time: 43.7 us -> 43.2 us (0.989)
  Pallas kernels: 43 us -> 42.4 us
    pallas_call x1, Pallas kernels: 40.6 us -> 40.1 us  [local(): pl.pallas_call(functools.partial(power_kernel, sizes), out_shape=(jax.Sha...]
where the time goes in v5:
time: 43.2 us; the launch traced here: 43.1 us
  Pallas kernels  42.4 us (98%)
  between operations  0.64 us (1%)
    pallas_call x1, Pallas kernels, local(): pl.pallas_call(functools.partial(power_kernel, sizes), out_shape=(jax.Sha...  40.1 us
    pallas_call x1, Pallas kernels, local(): pl.pallas_call(factor_kernel, out_shape=(jax.ShapeDtypeStruct(block, F32)...  2.38 us

profile of v5, /device:TPU:1, one launch (start us, length us, event | category | flops | bytes accessed | tf_op | source)
XLA Modules:
  0.0 43.1 jit_solution(4523064559669753422)
XLA Ops:
  0.6 40.1 %shard_map.50 = (f32[16,8,32,128]{3,2,1,0:T(8,128)S(1)}, f32[1,128]{1,0:T(1,128)S(1)}) custom-call(f32[4,8,32,128]{3,2,1,0:T(8,128)} %right_hbm.1, f32[4,8,32,128]{3,2,1,0:T(8,128)} %guess_hbm.1, f32[8,32,128]{2,1,0:T(8,128)} %diag_hbm.1), custom_call_target="tpu_custom_call" | custom-call | tf_op jit(solution)/shard_map/pallas_call | solution.py:400
  40.7 2.4 %shard_map.51 = (f32[16,8,32,128]{3,2,1,0:T(8,128)}, f32[16,16]{1,0:T(8,128)}) custom-call(f32[1,128]{1,0:T(1,128)S(1)} %get-tuple-element.4.total, f32[16,8,32,128]{3,2,1,0:T(8,128)S(1)} %get-tuple-element.5.basis), custom_call_target="tpu_custom_call" | custom-call | tf_op jit(solution)/shard_map/pallas_call | solution.py:437
